TPU v7x, 512 devices: a whole 4x4x16 slice. The times are simulated.
512 devices in a mesh: dp: 4 (over y), sx: 8 (over z_lo), sy: 16 (over z_hi, x, core).
Axes of the slice: x: 4, y: 4, z: 16 (z_hi: 2, z_lo: 8; z = z_hi * 8 + z_lo), core: 2. Of those that a mesh axis runs over, the one named last changes fastest.
Arguments:
- volume: bfloat16 [4, 4, 64, 128, 128], P('dp', None, 'sx', 'sy'), may hold values from -6 to 6
- cotangent: bfloat16 [4, 256, 8, 16, 16], P('dp', ('sx', 'sy')), may hold values from -0.119628906 to 0.119628906
- first_weight: bfloat16 [3, 3, 3, 4, 64], replicated, may hold values from -0.625 to 0.625
- second_weight: bfloat16 [3, 3, 3, 64, 64], replicated, may hold values from -0.15625 to 0.15625
- third_weight: bfloat16 [3, 3, 3, 64, 256], replicated, may hold values from -0.15625 to 0.15625
Outputs:
- grad_first: float32 [3, 3, 3, 4, 64], replicated
- grad_second: float32 [3, 3, 3, 64, 64], replicated
- grad_third: float32 [3, 3, 3, 64, 256], replicated
All inputs are finite; a program needn't handle non-finite values.
Results may differ from a plain program's by a relative error of at most 0.014.
Values may be sent and summed in bfloat16 or wider, within the bound.
A program may use at most 128 MiB of HBM per device.

v0:
```python
import jax
import jax.numpy as jnp
from jax import lax
from jax.sharding import PartitionSpec as P

LAYOUT = ("NCDHW", "DHWIO", "NCDHW")
ADJOINT_LAYOUT = ("NCDHW", "DHWOI", "NCDHW")


def passed_along(value, axis, steps):
    count = lax.axis_size(axis)
    leading, last = (max(0, -steps), min(count, count - steps))
    return lax.ppermute(value, axis, [(source, source + steps) for source in range(leading, last)])


def convolve(field, kernel, margins):
    return lax.conv_general_dilated(
        field,
        kernel,
        (2, 2, 2),
        margins,
        dimension_numbers=LAYOUT,
        preferred_element_type=jnp.float32,
    )


def kernel_grad(field, delta, margins):
    padded = jnp.pad(field, ((0, 0), (0, 0)) + tuple(margins))
    samples = field.shape[0]
    channels_in = field.shape[1]
    out_x, out_y, out_z = (delta.shape[2], delta.shape[3], delta.shape[4])
    tap_terms = []
    for shift_x in range(3):
        for shift_y in range(3):
            for shift_z in range(3):
                window = lax.slice(
                    padded,
                    (0, 0, shift_x, shift_y, shift_z),
                    (
                        samples,
                        channels_in,
                        shift_x + 2 * out_x - 1,
                        shift_y + 2 * out_y - 1,
                        shift_z + 2 * out_z - 1,
                    ),
                    (1, 1, 2, 2, 2),
                )
                tap_terms.append(
                    jnp.einsum("bcxyz,boxyz->co", window, delta, preferred_element_type=jnp.float32)
                )
    return jnp.stack(tap_terms).reshape(3, 3, 3, channels_in, delta.shape[1])


def adjoint(delta, kernel, lower_pads, lengths):
    borders = []
    for lower_pad, length, cell_count in zip(lower_pads, lengths, delta.shape[2:]):
        borders.append((2 - lower_pad, length + 1 + lower_pad - 2 * cell_count))
    flipped = kernel[::-1, ::-1, ::-1]
    return lax.conv_general_dilated(
        delta,
        flipped,
        (1, 1, 1),
        borders,
        lhs_dilation=(2, 2, 2),
        dimension_numbers=ADJOINT_LAYOUT,
        preferred_element_type=jnp.float32,
    )


def gelu_back(preact, upstream):
    return jax.vjp(jax.nn.gelu, preact)[1](upstream)[0]


def settle(values):
    return values.astype(jnp.bfloat16)


def rim_along_x(plane):
    return passed_along(plane, "sx", 1)


def rim_along_y(plane):
    return passed_along(plane, "sy", 1)


def late_rim_x(plane):
    return passed_along(plane, "sx", 1)


def late_rim_y(plane):
    return passed_along(plane, "sy", 1)


def extend(field, along_x, along_y):
    below = along_x(field[:, :, -1:])
    wider = jnp.concatenate([below, field], axis=2)
    beside = along_y(wider[:, :, :, -1:])
    return jnp.concatenate([beside, wider], axis=3)


def retract(gradient):
    upper_side = passed_along(gradient[:, :, :, :1].astype(jnp.bfloat16), "sy", -1).astype(
        jnp.float32
    )
    interior = gradient[:, :, :, 1:]
    interior = interior.at[:, :, :, -1:].add(upper_side)
    upper_row = passed_along(interior[:, :, :1].astype(jnp.bfloat16), "sx", -1).astype(jnp.float32)
    kept_cells = interior[:, :, 1:]
    return kept_cells.at[:, :, -1:].add(upper_row)


def to_blocks(values, blocks_x, blocks_y):
    samples, channels, extent_x, extent_y, extent_z = values.shape
    width_x = extent_x // blocks_x
    width_y = extent_y // blocks_y
    pieces = values.reshape(samples, channels, blocks_x, width_x, blocks_y, width_y, extent_z)
    pieces = pieces.transpose(2, 4, 0, 1, 3, 5, 6).reshape(
        blocks_x * blocks_y, samples, channels, width_x, width_y, extent_z
    )
    arrived = lax.all_to_all(pieces, ("sx", "sy"), split_axis=0, concat_axis=2, tiled=True)
    return arrived[0]


def local(volume, cotangent, first_weight, second_weight, third_weight):
    block_margins = ((0, 0), (0, 0), (1, 1))
    lower_block = (0, 0, 1)
    blocks_x = lax.axis_size("sx")
    blocks_y = lax.axis_size("sy")
    source = extend(volume, rim_along_x, rim_along_y)
    pre_first = convolve(source, first_weight, block_margins)
    act_first = settle(jax.nn.gelu(pre_first))
    padded_first = extend(act_first, rim_along_x, rim_along_y)
    pre_second = convolve(padded_first, second_weight, block_margins)
    act_second = settle(jax.nn.gelu(pre_second))
    padded_second = extend(act_second, late_rim_x, late_rim_y)
    upstream = to_blocks(cotangent, blocks_x, blocks_y)
    pre_third = convolve(padded_second, third_weight, block_margins)
    delta_third = settle(gelu_back(pre_third, upstream.astype(jnp.float32)))
    grad_third = kernel_grad(padded_second, delta_third, block_margins)
    back_padded = adjoint(delta_third, third_weight, lower_block, padded_second.shape[2:])
    back_second = retract(back_padded)
    delta_second = settle(gelu_back(pre_second, back_second))
    grad_second = kernel_grad(padded_first, delta_second, block_margins)
    back_first = retract(adjoint(delta_second, second_weight, lower_block, padded_first.shape[2:]))
    delta_first = settle(gelu_back(pre_first, back_first))
    grad_first = kernel_grad(source, delta_first, block_margins)
    return lax.psum((grad_first, grad_second, grad_third), ("dp", "sx", "sy"))


def solution(mesh):
    placed = (
        P("dp", None, "sx", "sy", None),
        P("dp", ("sx", "sy"), None, None, None),
        P(),
        P(),
        P(),
    )
    return jax.shard_map(
        local, mesh=mesh, in_specs=placed, out_specs=(P(), P(), P()), check_vma=False
    )
```

profile of v0, /device:TPU:1, one launch (start us, length us, event | category | flops | bytes accessed | tf_op | source)
XLA Modules:
  0.0 869.8 jit_solution(3003090617901127901)
XLA Ops:
  14.0 4.5 collective-permute-start.1
  39.9 33.2 %all-to-all-start = ((bf16[128,1,2,1,1,16]{5,2,4,3,1,0:T(2,128)(2,1)}), bf16[128,1,2,1,1,16]{5,2,4,3,1,0:T(2,128)(2,1)S(1)}, u32[]{:S(2)}, u32[]{:S(2)}) async-start(bf16[128,1,2,1,1,16]{5,2,4,3,1,0:T(2,128)(2,1)} %bitcast.3), calls=%async_computation | async-start | bytes 131072 | tf_op jit(solution)/shard_map/all_to_all | solution.py:120
  81.0 4.5 collective-permute-start.5
  85.7 6.0 slice.458
  91.7 6.0 slice.475
  97.6 6.0 slice.476
  103.6 6.0 slice.477
  109.6 5.9 slice.478
  115.5 6.0 slice.479
  121.4 5.9 slice.480
  127.4 6.0 slice.481
  133.3 5.9 slice.482
  139.3 6.0 slice.483
  145.2 6.0 slice.484
  151.2 6.0 slice.485
  157.2 6.0 slice.486
  163.2 5.9 slice.487
  169.1 5.9 slice.488
  175.0 5.9 slice.489
  180.9 6.0 slice.490
  186.9 5.9 slice.491
  192.8 5.9 slice.492
  198.7 5.9 slice.493
  204.6 5.9 slice.494
  210.5 5.9 slice.495
  216.4 6.0 slice.496
  222.4 5.9 slice.497
  228.3 5.9 slice.498
  234.2 5.9 slice.499
  240.2 6.0 slice.500
  377.1 120.7 %psum.21 = f32[3,3,3,4,64]{4,3,2,1,0:T(4,128)} all-reduce(f32[3,3,3,4,64]{4,3,2,1,0:T(4,128)S(1)} %bitcast.1140), channel_id=1, replica_groups=mesh['dp'=4,'sx'=8,'sy'=16] {'dp','sx','sy'}, use_global_device_ids=true, to_apply=%region_0.1 | all-reduce | flops 6912 | bytes 55296 | tf_op jit(solution)/shard_map/psum | solution.py:147
  497.7 361.6 %all-reduce.6.cloned.1.call-done = (f32[3,3,3,64,64]{4,3,2,1,0:T(8,128)}, f32[3,3,3,64,256]{4,3,2,1,0:T(8,128)}) async-done(((f32[3,3,3,64,64]{4,3,2,1,0:T(8,128)}, f32[3,3,3,64,256]{4,3,2,1,0:T(8,128)}), (f32[3,3,3,64,64]{4,3,2,1,0:T(8,128)}, f32[3,3,3,64,256]{4,3,2,1,0:T(8,128)})) %all-reduce.6.cloned.1.call-update) | async-done | bytes 2211856 | tf_op jit(solution)/shard_map/psum | solution.py:147
  (349 shorter events, 169.6 us)
Async XLA Ops:
  7.2 281.4 %copy-start = (bf16[3,3,3,64,256]{4,3,2,1,0:T(8,128)(2,1)S(1)}, bf16[3,3,3,64,256]{4,3,2,1,0:T(8,128)(2,1)}, u32[]{:S(2)}) copy-start(bf16[3,3,3,64,256]{4,3,2,1,0:T(8,128)(2,1)} %param.17) | copy-start | bytes 2654212
  8.0 5.1 collective-permute-start
  14.0 6.3 collective-permute-start.1
  29.9 5.2 collective-permute-start.2
  35.1 38.0 %collective-permute-start.3 = (bf16[1,64,5,1,64]{1,4,3,2,0:T(8,128)(2,1)S(1)}, bf16[1,64,5,1,64]{1,4,3,2,0:T(8,128)(2,1)S(1)}, u32[]{:S(2)}, u32[]{:S(2)}) collective-permute-start(bf16[1,64,5,1,64]{1,4,3,2,0:T(8,128)(2,1)S(1)} %pad_maximum_fusion.1), channel_id=1, source_target_pairs={{0,1},{1,2},{2,3},{3,4},{4,5},{5,6},{6,7},{7,8},{8,9},{9,10},{10,1... | collective-permute-start | bytes 122888 | tf_op jit(solution)/shard_map/ppermute | solution.py:13
  39.9 211.5 %all-to-all-start = ((bf16[128,1,2,1,1,16]{5,2,4,3,1,0:T(2,128)(2,1)}), bf16[128,1,2,1,1,16]{5,2,4,3,1,0:T(2,128)(2,1)S(1)}, u32[]{:S(2)}, u32[]{:S(2)}) async-start(bf16[128,1,2,1,1,16]{5,2,4,3,1,0:T(2,128)(2,1)} %bitcast.3), calls=%async_computation | async-start | bytes 131072 | tf_op jit(solution)/shard_map/all_to_all | solution.py:120
  73.1 786.3 %all-reduce.6.cloned.1.call-start = ((), (), s32[]{:S(2)}) async-start(), calls=%async_computation.1 | async-start | bytes 5308416 | tf_op jit(solution)/shard_map/psum | solution.py:147
  76.2 4.2 collective-permute-start.4
  81.0 168.4 %copy-start.5 = (f32[4,4,8,9,64]{4,2,3,1,0:T(8,128)S(1)}, f32[4,4,8,9,64]{4,2,3,1,0:T(8,128)}, u32[]{:S(2)}) copy-start(f32[4,4,8,9,64]{4,2,3,1,0:T(8,128)} %get-tuple-element.95) | copy-start | bytes 884740
  81.0 207.3 %collective-permute-start.5 = (bf16[1,64,3,1,32]{1,3,4,2,0:T(2,128)(2,1)}, bf16[1,64,3,1,32]{1,3,4,2,0:T(2,128)(2,1)S(1)}, u32[]{:S(2)}, u32[]{:S(2)}) collective-permute-start(bf16[1,64,3,1,32]{1,3,4,2,0:T(2,128)(2,1)} %pad_maximum_fusion.2), channel_id=1, source_target_pairs={{0,1},{1,2},{2,3},{3,4},{4,5},{5,6},{6,7},{7,8},{8,9},{9,10},{10,1... | collective-permute-start | bytes 36872 | tf_op jit(solution)/shard_map/ppermute | solution.py:13
  250.4 35.8 %copy-start.20 = (f32[2,2,8,5,64]{4,2,3,1,0:T(8,128)S(1)}, f32[2,2,8,5,64]{4,2,3,1,0:T(8,128)}, u32[]{:S(2)}) copy-start(f32[2,2,8,5,64]{4,2,3,1,0:T(8,128)} %get-tuple-element.91) | copy-start | bytes 122884
  250.4 35.9 %copy-start.19 = (f32[2,2,8,5,64]{4,2,3,1,0:T(8,128)S(1)}, f32[2,2,8,5,64]{4,2,3,1,0:T(8,128)}, u32[]{:S(2)}) copy-start(f32[2,2,8,5,64]{4,2,3,1,0:T(8,128)} %get-tuple-element.90) | copy-start | bytes 122884
  251.4 35.6 %copy-start.18 = (f32[2,2,8,5,64]{4,2,3,1,0:T(8,128)S(1)}, f32[2,2,8,5,64]{4,2,3,1,0:T(8,128)}, u32[]{:S(2)}) copy-start(f32[2,2,8,5,64]{4,2,3,1,0:T(8,128)} %get-tuple-element.88) | copy-start | bytes 122884
  251.6 37.0 %copy-start.55 = (pred[8,3]{0,1:T(4,128)(4,1)S(1)}, pred[8,3]{0,1:T(4,128)(4,1)}, u32[]{:S(2)}) copy-start(pred[8,3]{0,1:T(4,128)(4,1)} %constant.166) | copy-start | bytes 76
  292.1 21.0 %copy-start.50 = (bf16[1,64,1,1,16]{1,3,4,2,0:T(2,128)(2,1)S(1)}, bf16[1,64,1,1,16]{1,3,4,2,0:T(2,128)(2,1)}, u32[]{:S(2)}) copy-start(bf16[1,64,1,1,16]{1,3,4,2,0:T(2,128)(2,1)} %get-tuple-element.61) | copy-start | bytes 6148
  292.1 21.2 %copy-start.49 = (bf16[1,64,1,1,16]{1,3,4,2,0:T(2,128)(2,1)S(1)}, bf16[1,64,1,1,16]{1,3,4,2,0:T(2,128)(2,1)}, u32[]{:S(2)}) copy-start(bf16[1,64,1,1,16]{1,3,4,2,0:T(2,128)(2,1)} %get-tuple-element.60) | copy-start | bytes 6148
  292.1 21.4 %collective-permute-start.6 = (bf16[1,64,3,1,32]{1,3,4,2,0:T(2,128)(2,1)S(1)}, bf16[1,64,3,1,32]{1,3,4,2,0:T(2,128)(2,1)S(1)}, u32[]{:S(2)}, u32[]{:S(2)}) collective-permute-start(bf16[1,64,3,1,32]{1,3,4,2,0:T(2,128)(2,1)S(1)} %slice_bitcast_fusion.12), channel_id=1, source_target_pairs={{1,0},{2,1},{3,2},{4,3},{5,4},{6,5},{7,6},{8,7},{9,8},{10,9},{11,1... | collective-permute-start | bytes 36872 | tf_op jit(solution)/shard_map/ppermute | solution.py:13
  317.0 5.1 collective-permute-start.7
  326.5 25.7 %copy-start.17 = (bf16[1,64,2,2,32]{1,4,3,2,0:T(8,128)(2,1)S(1)}, bf16[1,64,2,2,32]{1,4,3,2,0:T(8,128)(2,1)}, u32[]{:S(2)}) copy-start(bf16[1,64,2,2,32]{1,4,3,2,0:T(8,128)(2,1)} %slice.516) | copy-start | bytes 49156
  326.5 26.4 %copy-start.16 = (bf16[1,64,2,2,32]{1,4,3,2,0:T(8,128)(2,1)S(1)}, bf16[1,64,2,2,32]{1,4,3,2,0:T(8,128)(2,1)}, u32[]{:S(2)}) copy-start(bf16[1,64,2,2,32]{1,4,3,2,0:T(8,128)(2,1)} %slice.517) | copy-start | bytes 49156
  326.5 27.2 %copy-start.15 = (bf16[1,64,2,2,32]{1,4,3,2,0:T(8,128)(2,1)S(1)}, bf16[1,64,2,2,32]{1,4,3,2,0:T(8,128)(2,1)}, u32[]{:S(2)}) copy-start(bf16[1,64,2,2,32]{1,4,3,2,0:T(8,128)(2,1)} %slice.518) | copy-start | bytes 49156
  326.5 28.0 %copy-start.14 = (bf16[1,64,2,2,32]{1,4,3,2,0:T(8,128)(2,1)S(1)}, bf16[1,64,2,2,32]{1,4,3,2,0:T(8,128)(2,1)}, u32[]{:S(2)}) copy-start(bf16[1,64,2,2,32]{1,4,3,2,0:T(8,128)(2,1)} %slice.519) | copy-start | bytes 49156
  326.6 28.8 %copy-start.13 = (bf16[1,64,2,2,32]{1,4,3,2,0:T(8,128)(2,1)S(1)}, bf16[1,64,2,2,32]{1,4,3,2,0:T(8,128)(2,1)}, u32[]{:S(2)}) copy-start(bf16[1,64,2,2,32]{1,4,3,2,0:T(8,128)(2,1)} %slice.520) | copy-start | bytes 49156
  326.6 29.6 %copy-start.12 = (bf16[1,64,2,2,32]{1,4,3,2,0:T(8,128)(2,1)S(1)}, bf16[1,64,2,2,32]{1,4,3,2,0:T(8,128)(2,1)}, u32[]{:S(2)}) copy-start(bf16[1,64,2,2,32]{1,4,3,2,0:T(8,128)(2,1)} %slice.521) | copy-start | bytes 49156
  326.6 30.4 %copy-start.11 = (bf16[1,64,2,2,32]{1,4,3,2,0:T(8,128)(2,1)S(1)}, bf16[1,64,2,2,32]{1,4,3,2,0:T(8,128)(2,1)}, u32[]{:S(2)}) copy-start(bf16[1,64,2,2,32]{1,4,3,2,0:T(8,128)(2,1)} %slice.522) | copy-start | bytes 49156
  326.6 31.2 %copy-start.10 = (bf16[1,64,2,2,32]{1,4,3,2,0:T(8,128)(2,1)S(1)}, bf16[1,64,2,2,32]{1,4,3,2,0:T(8,128)(2,1)}, u32[]{:S(2)}) copy-start(bf16[1,64,2,2,32]{1,4,3,2,0:T(8,128)(2,1)} %slice.523) | copy-start | bytes 49156
  326.6 31.9 %copy-start.9 = (bf16[1,64,2,2,32]{1,4,3,2,0:T(8,128)(2,1)S(1)}, bf16[1,64,2,2,32]{1,4,3,2,0:T(8,128)(2,1)}, u32[]{:S(2)}) copy-start(bf16[1,64,2,2,32]{1,4,3,2,0:T(8,128)(2,1)} %slice.524) | copy-start | bytes 49156
  326.6 32.7 %copy-start.8 = (bf16[1,64,2,2,32]{1,4,3,2,0:T(8,128)(2,1)S(1)}, bf16[1,64,2,2,32]{1,4,3,2,0:T(8,128)(2,1)}, u32[]{:S(2)}) copy-start(bf16[1,64,2,2,32]{1,4,3,2,0:T(8,128)(2,1)} %slice.525) | copy-start | bytes 49156
  326.6 33.5 %copy-start.7 = (bf16[1,64,2,2,32]{1,4,3,2,0:T(8,128)(2,1)S(1)}, bf16[1,64,2,2,32]{1,4,3,2,0:T(8,128)(2,1)}, u32[]{:S(2)}) copy-start(bf16[1,64,2,2,32]{1,4,3,2,0:T(8,128)(2,1)} %slice.526) | copy-start | bytes 49156
  326.8 34.4 %collective-permute-start.8 = (bf16[1,64,5,1,64]{1,3,4,2,0:T(2,128)(2,1)S(1)}, bf16[1,64,5,1,64]{1,3,4,2,0:T(2,128)(2,1)S(1)}, u32[]{:S(2)}, u32[]{:S(2)}) collective-permute-start(bf16[1,64,5,1,64]{1,3,4,2,0:T(2,128)(2,1)S(1)} %slice_bitcast_fusion.5), channel_id=1, source_target_pairs={{1,0},{2,1},{3,2},{4,3},{5,4},{6,5},{7,6},{8,7},{9,8},{10,9},{11,1... | collective-permute-start | bytes 122888 | tf_op jit(solution)/shard_map/ppermute | solution.py:13
  341.3 24.9 %copy-start.6 = (bf16[1,64,2,2,32]{1,4,3,2,0:T(8,128)(2,1)S(1)}, bf16[1,64,2,2,32]{1,4,3,2,0:T(8,128)(2,1)}, u32[]{:S(2)}) copy-start(bf16[1,64,2,2,32]{1,4,3,2,0:T(8,128)(2,1)} %slice.527) | copy-start | bytes 49156
  364.9 5.0 collective-permute-start.9
  (39 other events, 168.6 us)
Sparse Core Ops, SparseCore 0:
  367.2 492.1 all-reduce.5
where the time goes:
time: 874 us; the launch traced here: 870 us
  waiting for transfers between devices  371 us (42%)
  local copies, waits for them, and re-layouts  226 us (26%)
  blocking collectives  121 us (14%)
  matrix products  67.3 us (8%)
  starting transfers between devices  64.6 us (7%)
  between operations  15.2 us (2%)
    psum x1, waiting for transfers between devices, local(): return lax.psum((grad_first, grad_second, grad_third), ('dp', 'sx', 'sy'))  362 us
    slice x56, local copies, waits for them, and re-layouts, kernel_grad(): lax.slice(padded, (0, 0, shift_x, shift_y, shift_z), (samples, channels_i...  197 us
    psum x1, blocking collectives, local(): return lax.psum((grad_first, grad_second, grad_third), ('dp', 'sx', 'sy'))  121 us
    dot_general x81, matrix products, kernel_grad(): jnp.einsum('bcxyz,boxyz->co', window, delta, preferred_element_type=jnp.f...  58 us
    all_to_all x1, starting transfers between devices, to_blocks(): lax.all_to_all(pieces, ('sx', 'sy'), split_axis=0, concat_axis=2, tiled=T...  33.2 us
    ppermute x10, starting transfers between devices, passed_along(): lax.ppermute(value, axis, [(source, source + steps) for source in range(l...  31.3 us
  transfers between devices with their start and end apart: 12, of which 7 were waited for; matrix products, arithmetic and copies ran while one was open for 31% of the time, Pallas kernels for 0%

commit v1 on v0

v1 whole, which is shorter than its diff:
```python
import functools

import jax
import jax.numpy as jnp
import numpy as np
from jax import lax
from jax.experimental import pallas as pl
from jax.experimental.pallas import tpu as pltpu
from jax.sharding import PartitionSpec as P

MESH = pl.DeviceIdType.MESH
LOW, WIDE = jnp.bfloat16, jnp.float32
CORES = 2
ROWS, LANES = 16, 128
SLOT = 40
FIRST_UNITS, SECOND_UNITS, THIRD_UNITS = 8, 56, 216
OWN = ((0, 0), (0, 1), (1, 0), (1, 1))
CELLS = [(1 + a, 1 + b) for a, b in OWN] + [(0, 0), (0, 1), (0, 2), (1, 0), (2, 0)]


def selection():
    result = np.zeros((3, 2, 2, 4, 16, 7, LANES), np.float32)
    for offset in range(3):
        for dx, (pair, odd) in enumerate(((1, 1), (0, 0), (0, 1))):
            for channel in range(4):
                for cell in range(7):
                    for dy in range(3):
                        lane = offset * SLOT + (dx * 3 + dy) * 4 + channel
                        result[offset, pair, odd, channel, 2 * cell + dy + 1, cell, lane] = 1
    return result.reshape(768, 7 * LANES)


def gelu_parts(v):
    square = v * v
    t = jnp.tanh(np.sqrt(2 / np.pi) * (v + 0.044715 * (v * square)))
    return t, square


def gelu(v):
    t, _ = gelu_parts(v)
    return 0.5 * v * (1 + t)


def gelu_slope(v):
    t, square = gelu_parts(v)
    return 0.5 * (1 + t) + 0.5 * v * (1 - t * t) * (np.sqrt(2 / np.pi) * (1 + 3 * 0.044715 * square))


def dot(a, b, transposed=False):
    return lax.dot_general(a, b, (((1,), (1 if transposed else 0,)), ((), ())), preferred_element_type=WIDE)


def down(v, period):
    row = lax.broadcasted_iota(jnp.int32, v.shape, 0)
    return jnp.where((row & (period - 1)) == 0, 0.0, pltpu.roll(v, 1, axis=0))


def up(v):
    row = lax.broadcasted_iota(jnp.int32, v.shape, 0)
    return jnp.where(row == v.shape[0] - 1, 0.0, pltpu.roll(v, v.shape[0] - 1, axis=0))


class Place:
    def __init__(self, dp, sx, sy):
        self.chips_x = min(4, sy // CORES)
        self.low_z, self.chips_y = sx, dp
        self.plane = self.chips_x * dp
        self.depth = sx * (sy // (CORES * self.chips_x))
        self.y, self.sx, self.sy = (lax.axis_index(name) for name in ("dp", "sx", "sy"))
        self.core = lax.rem(self.sy, CORES)
        self.p = lax.rem(self.sy // CORES, self.chips_x) * dp + self.y
        self.z = (self.sy // (CORES * self.chips_x)) * sx + self.sx

    def device(self, core=None, p=None, z=None):
        core = self.core if core is None else core
        p = self.p if p is None else p
        z = self.z if z is None else z
        chip_x, y = p // self.chips_y, lax.rem(p, self.chips_y)
        high, low = z // self.low_z, lax.rem(z, self.low_z)
        return (y, low, (high * self.chips_x + chip_x) * CORES + core)


def others(count, me, body):
    def step(distance, carry):
        body(lax.rem(me + distance, count))
        return carry

    lax.fori_loop(1, count, step, 0)


def copy(source, target, sems, at, there, device):
    return pltpu.make_async_remote_copy(
        src_ref=source, dst_ref=target, send_sem=sems.at[0, at], recv_sem=sems.at[1, there],
        device_id=device, device_id_type=MESH)


class Reduction:
    def __init__(self, here, grads, refs):
        self.here, self.grads = here, grads
        (self.half_out, self.half_in, self.plane_out, self.plane_in, self.depth_out, self.depth_in,
         self.final, self.gathered, self.half_sems, self.plane_sems, self.depth_sems, self.final_sems,
         self.gather_sems, self.pair_sems) = refs
        self.share = self.plane_out.shape[1]
        self.half = here.plane * self.share
        self.partner = here.device(core=1 - here.core)
        owners = [unit * here.depth // self.share for unit in range(self.share)]
        self.owned = [(unit, owner, unit - owners.index(owner)) for unit, owner in enumerate(owners)]

    @staticmethod
    def scratch(units, plane, depth):
        share = units // (CORES * plane)
        slots = -(-share // depth)
        unit = (ROWS, LANES)
        return [
            pltpu.VMEM((plane * share, *unit), LOW),
            pltpu.VMEM((plane * share, *unit), LOW),
            pltpu.VMEM((plane, share, *unit), LOW),
            pltpu.VMEM((plane, share, *unit), LOW),
            pltpu.VMEM((share, *unit), LOW),
            pltpu.VMEM((slots, depth, *unit), LOW),
            pltpu.VMEM((share, *unit), LOW),
            pltpu.VMEM((CORES, plane, share, *unit), LOW),
            pltpu.SemaphoreType.DMA((2, 1)),
            pltpu.SemaphoreType.DMA((2, plane)),
            pltpu.SemaphoreType.DMA((2, max(share, slots * depth))),
            pltpu.SemaphoreType.DMA((2, max(share, slots * depth))),
            pltpu.SemaphoreType.DMA((2, plane)),
            pltpu.SemaphoreType.DMA((2, plane)),
        ]

    def swap(self):
        return copy(self.half_out, self.half_in, self.half_sems, 0, 0, self.partner)

    def start_swap(self):
        self.half_out[...] = self.grads[pl.ds((1 - self.here.core) * self.half, self.half)].astype(LOW)
        self.swap().start()

    def to_plane(self, q, source_slot):
        here = self.here
        return copy(self.plane_out.at[q], self.plane_in.at[source_slot], self.plane_sems, q, source_slot, here.device(p=q))

    def start_plane(self):
        here = self.here
        self.swap().wait()
        mine = self.grads[pl.ds(here.core * self.half, self.half)]
        self.plane_out[...] = (mine + self.half_in[...].astype(WIDE)).astype(LOW).reshape(self.plane_out.shape)
        others(here.plane, here.p, lambda q: self.to_plane(q, here.p).start())

    def to_depth(self, unit, owner, slot, q):
        here = self.here
        return copy(self.depth_out.at[unit], self.depth_in.at[slot, q], self.depth_sems, unit,
                    slot * here.depth + q, here.device(z=owner))

    def start_depth(self):
        here = self.here
        self.plane_in[here.p] = self.plane_out[here.p]
        others(here.plane, here.p, lambda q: self.to_plane(q, q).wait())
        self.depth_out[...] = jnp.sum(self.plane_in[...].astype(WIDE), axis=0).astype(LOW)
        for unit, owner, slot in self.owned:
            @pl.when(here.z != owner)
            def _():
                self.to_depth(unit, owner, slot, here.z).start()

    def to_final(self, unit, slot, q):
        here = self.here
        return copy(self.final.at[unit], self.final.at[unit], self.final_sems, slot * here.depth + q, unit, here.device(z=q))

    def start_final(self):
        here = self.here
        for unit, owner, slot in self.owned:
            @pl.when(here.z == owner)
            def _():
                self.depth_in[slot, owner] = self.depth_out[unit]
                others(here.depth, here.z, lambda q: self.to_depth(unit, q, slot, q).wait_recv())
                self.final[unit] = jnp.sum(self.depth_in[slot].astype(WIDE), axis=0).astype(LOW)
                others(here.depth, here.z, lambda q: self.to_final(unit, slot, q).start())

    def to_gather(self, q, source_slot):
        here = self.here
        return copy(self.final, self.gathered.at[here.core, source_slot], self.gather_sems, q, source_slot, here.device(p=q))

    def to_pair(self, core, q):
        return copy(self.gathered.at[core, q], self.gathered.at[core, q], self.pair_sems, q, q, self.partner)

    def start_gather(self):
        here = self.here
        for unit, owner, slot in self.owned:
            @pl.when(here.z != owner)
            def _():
                self.to_depth(unit, owner, slot, here.z).wait_send()
                self.to_final(unit, slot, owner).wait_recv()

        others(here.plane, here.p, lambda q: self.to_gather(q, here.p).start())
        self.gathered[here.core, here.p] = self.final[...]
        self.to_pair(here.core, here.p).start()

    def pass_on(self):
        here = self.here

        def step(q):
            self.to_gather(q, q).wait_recv()
            self.to_pair(here.core, q).start()

        others(here.plane, here.p, step)

    def finish(self):
        here = self.here
        for unit, owner, slot in self.owned:
            @pl.when(here.z == owner)
            def _():
                others(here.depth, here.z, lambda q: self.to_final(unit, slot, q).wait_send())

        others(here.plane, here.p, lambda q: self.to_gather(q, q).wait_send())

        def arrived(q, carry):
            self.to_pair(1 - here.core, q).wait()
            return carry

        lax.fori_loop(0, here.plane, arrived, 0)
        return self.gathered[...].reshape(-1, ROWS, LANES)


class Halo:
    def __init__(self, here, sizes, step, sems, first, triples):
        self.items = []
        for index, (along_x, along_y, source, target) in enumerate(triples):
            sends = receives = None
            for along, place, size in ((along_x, here.sx, sizes[1]), (along_y, here.sy, sizes[2])):
                if not along:
                    continue
                ahead, behind = place < size - 1, place > 0
                send, receive = (ahead, behind) if step > 0 else (behind, ahead)
                sends = send if sends is None else jnp.logical_and(sends, send)
                receives = receive if receives is None else jnp.logical_and(receives, receive)
            device = (here.y, here.sx + step * along_x, here.sy + step * along_y)
            move = copy(source, target, sems, first + index, first + index, device)
            self.items.append((sends, receives, move, target))

    def start(self):
        for sends, _, move, _ in self.items:
            @pl.when(sends)
            def _():
                move.start()

    def wait(self):
        for _, receives, move, target in self.items:
            @pl.when(receives)
            def _():
                move.wait_recv()

            @pl.when(jnp.logical_not(receives))
            def _():
                target[...] = jnp.zeros(target.shape, target.dtype)

    def sent(self):
        for sends, _, move, _ in self.items:
            @pl.when(sends)
            def _():
                move.wait_send()


def kernel(sizes, volume, cotangent, w1, w2, w3, select, out1, out2, out3,
           vx, vy, vc, w1c, w2s, w3s, sel, local_sems, halo_sems, r1, r1_sems, s2, r2, r2_sems,
           dts, xoff, c1, g1, act1, act1s, lhs2, pre2, g2, g2y, g2x_in, g2y_in, g2c_in, lhs3, d3, d3x, d3y, d3c,
           lhs2t, c1t, d2s, d1, grads_a, grads_b, *reductions):
    here = Place(*sizes)
    _, size_x, size_y = sizes
    kept = cotangent.shape[0]

    loads = [
        pltpu.make_async_copy(select, sel, local_sems.at[0]),
        pltpu.make_async_copy(w2.at[:, :, pl.ds(1, 2)], w2s.at[:, :, pl.ds(0, 2)], local_sems.at[1]),
        pltpu.make_async_copy(w2.at[:, :, pl.ds(0, 1)], w2s.at[:, :, pl.ds(3, 1)], local_sems.at[2]),
        pltpu.make_async_copy(w3.at[:, :, pl.ds(1, 2)], w3s.at[:, :, pl.ds(0, 2)], local_sems.at[3]),
        pltpu.make_async_copy(w3.at[:, :, pl.ds(0, 1)], w3s.at[:, :, pl.ds(3, 1)], local_sems.at[4]),
    ]
    for load in loads:
        load.start()

    barrier = pltpu.get_barrier_semaphore()

    def greet(device):
        pl.semaphore_signal(barrier, inc=1, device_id=device, device_id_type=MESH)

    lower = jnp.logical_and(here.sx > 0, here.sy > 0)
    upper = jnp.logical_and(here.sx < size_x - 1, here.sy < size_y - 1)
    others(here.depth, here.z, lambda q: greet(here.device(z=q)))
    others(size_y, here.sy, lambda q: greet((here.y, here.sx, q)))
    others(here.plane, here.p, lambda q: greet(here.device(p=q)))

    @pl.when(lower)
    def _():
        greet((here.y, here.sx - 1, here.sy - 1))

    @pl.when(upper)
    def _():
        greet((here.y, here.sx + 1, here.sy + 1))

    pl.semaphore_wait(barrier, here.depth + size_y + here.plane - 3 + lower.astype(jnp.int32) + upper.astype(jnp.int32))

    volumes = Halo(here, sizes, 1, halo_sems, 0, ((1, 0, volume, vx), (0, 1, volume, vy), (1, 1, volume, vc)))
    volumes.start()

    def to_rows(q, source_slot):
        return copy(cotangent.at[:, q], r1.at[source_slot], r1_sems, q, source_slot, (here.y, q, here.sy))

    others(size_x, here.sx, lambda q: to_rows(q, here.sx).start())
    r1[here.sx] = cotangent[:, here.sx]

    w1c[...] = jnp.zeros(w1c.shape, WIDE)
    blank = jnp.zeros((4, 64), WIDE)
    for offset in range(5):
        base = offset * SLOT if offset < 3 else 128 + (offset - 3) * SLOT
        for dx in range(3):
            for dy in range(3):
                left = w1[dx, dy, offset].astype(WIDE) if offset <= 2 else blank
                right = w1[dx, dy, offset - 2].astype(WIDE) if offset >= 2 else blank
                w1c[pl.ds(base + (dx * 3 + dy) * 4, 4), :] = jnp.concatenate([left, right], axis=1)
    for ref in (w2s, w3s):
        ref[:, :, 2] = jnp.zeros((3, 3, *ref.shape[3:]), LOW)
    for index in range(8):
        dts[index, 0:8, :] = jnp.zeros((8, 128), WIDE)

    others(size_x, here.sx, lambda q: to_rows(q, q).wait())
    groups = size_x * kept
    spread = groups * ROWS
    lane = lax.broadcasted_iota(jnp.int32, (ROWS, spread), 1)
    row = lax.broadcasted_iota(jnp.int32, (ROWS, spread), 0)
    repeat = jnp.where((lane & (ROWS - 1)) == row, 1.0, 0.0).astype(LOW)
    wide = dot(r1[...].reshape(groups * size_y, ROWS), repeat).reshape(groups, size_y, spread)
    lane = lax.broadcasted_iota(jnp.int32, wide.shape, 2)
    group = lax.broadcasted_iota(jnp.int32, wide.shape, 0)
    strips = jnp.sum(jnp.where((lane >> 4) == group, wide, 0.0), axis=0)
    s2[...] = jnp.broadcast_to(strips[:, None, :], s2.shape)

    def to_cell(q, source_slot):
        return copy(s2.at[q], r2.at[source_slot], r2_sems, q, source_slot, (here.y, here.sx, q))

    others(size_y, here.sy, lambda q: to_cell(q, here.sy).start())
    r2[here.sy] = s2[here.sy]

    loads[0].wait()
    volumes.wait()

    for pair in range(8):
        before, inside = (vc, vx) if pair < 4 else (vy, volume)
        tiles = []
        for odd in range(2):
            x = (2 * pair + odd) % 8
            for channel in range(4):
                tiles += [before[channel, x].astype(WIDE), inside[channel, x].astype(WIDE)]
        dts[pair, 8:136, :] = jnp.concatenate(tiles, axis=0).T
    for offset in range(5):
        for pair in range(8):
            xoff[offset, pair * 32:(pair + 1) * 32, :] = dts[pair, pl.ds(7 + offset, 32, stride=4), :].astype(LOW)
    for part, offsets in enumerate(((0, 1, 2), (3, 4))):
        blocks = []
        for offset in offsets:
            blocks += [xoff[offset, 32:256, :], xoff[offset, 0:224, :]]
        chosen = dot(jnp.concatenate(blocks, axis=1), sel[0:256 * len(offsets), :])
        for cell in range(7):
            c1[cell, :, part * 128:(part + 1) * 128] = chosen[:, cell * 128:(cell + 1) * 128].astype(LOW)
    first = w1c[...].astype(LOW)
    for cell in range(7):
        pre = dot(c1[cell], first)
        if cell >= 3:
            g1[cell - 3] = gelu_slope(pre[96:224])
        act = gelu(pre)
        act1[cell] = act.astype(LOW)
        act1s[cell] = down(act, 32).astype(LOW)

    for index, (x, y) in enumerate(CELLS):
        for dx in range(3):
            for dy in range(3):
                at = (dx * 3 + dy) * 256
                rows = slice((2 * x + dx) * 32, (2 * x + dx + 1) * 32)
                lhs2[index * 32:(index + 1) * 32, at:at + 128] = act1[2 * y + dy, rows, :]
                lhs2[index * 32:(index + 1) * 32, at + 128:at + 256] = act1s[2 * y + dy, rows, :]
    for load in loads[1:3]:
        load.wait()
    second = w2s[...].reshape(2304, 64)
    pre2[...] = dot(lhs2[...], second)
    for index, (x, y) in enumerate(CELLS):
        pre = jnp.concatenate(
            [pre2[pl.ds(index * 32 + parity, 16, stride=2), :] for parity in range(2)], axis=1)
        if index < 4:
            slope = gelu_slope(pre)
            g2[index] = slope
            if index in (0, 2):
                g2y[index // 2] = slope
        act = gelu(pre)
        at = (x * 3 + y) * 256
        lhs3[:, at:at + 128] = act
        lhs3[:, at + 128:at + 256] = down(act, 16)
    slopes = Halo(here, sizes, -1, halo_sems, 3, (
        (1, 0, g2.at[pl.ds(0, 2)], g2x_in), (0, 1, g2y, g2y_in), (1, 1, g2.at[pl.ds(0, 1)], g2c_in)))
    slopes.start()

    others(size_y, here.sy, lambda q: to_cell(q, q).wait())
    strips = jnp.max(r2[...], axis=1).T.astype(LOW)
    channel = lax.broadcasted_iota(jnp.int32, (size_y, 256), 1)
    owner = lax.broadcasted_iota(jnp.int32, (size_y, 256), 0)
    choose = jnp.where(lax.rem(channel // kept, size_y) == owner, 1.0, 0.0).astype(LOW)
    wide = dot(strips, choose).reshape(groups, ROWS, 256)
    channel = lax.broadcasted_iota(jnp.int32, wide.shape, 2)
    group = lax.broadcasted_iota(jnp.int32, wide.shape, 0)
    mine = (channel // (kept * size_y)) * kept + lax.rem(channel, kept) == group
    upstream = jnp.sum(jnp.where(mine, wide, 0.0), axis=0)
    for load in loads[3:5]:
        load.wait()
    third = w3s[...].reshape(2304, 256)
    pre = dot(lhs3[...].astype(LOW), third)
    delta = (gelu_slope(pre) * upstream).astype(LOW)
    d3[...] = delta
    deltas = Halo(here, sizes, -1, halo_sems, 6, ((1, 0, d3, d3x), (0, 1, d3, d3y), (1, 1, d3, d3c)))
    deltas.start()

    for tap in range(9):
        turned = lhs3[:, tap * 256:(tap + 1) * 256].T.astype(LOW)
        grad = dot(turned, delta)
        for dz, rows in enumerate((192, 0, 64)):
            for lanes in range(2):
                at = lanes * 108 + (tap * 3 + dz) * 4
                grads_a[at:at + 4] = grad[rows:rows + 64, lanes * 128:(lanes + 1) * 128].reshape(4, ROWS, LANES)
    spare = grads_a.shape[0] - THIRD_UNITS
    if spare:
        grads_a[THIRD_UNITS:] = jnp.zeros((spare, ROWS, LANES), WIDE)
    many = len(reductions) // 2
    large = Reduction(here, grads_a, reductions[:many])
    small = Reduction(here, grads_b, reductions[many:])
    large.start_swap()

    for block in range(18):
        lhs2t[block * 128:(block + 1) * 128, :] = lhs2[0:128, block * 128:(block + 1) * 128].astype(WIDE).T.astype(LOW)
    for cell in range(4):
        for half in range(2):
            lanes = slice(half * 128, (half + 1) * 128)
            c1t[lanes, cell * 128:(cell + 1) * 128] = c1[3 + cell, 96:224, lanes].astype(WIDE).T.astype(LOW)

    large.start_plane()
    slopes.wait()
    deltas.wait()

    sources = {(0, 0): 0, (1, 0): 1, (0, 1): 2, (1, 1): 3}
    back = dot(jnp.concatenate([d3[...], d3x[...], d3y[...], d3c[...]], axis=0), third, transposed=True)
    reads = {0: ((0, 1),), 1: ((0, 2), (1, 0)), 2: ((1, 1),)}
    slope_at = {(0, 0): g2.at[0], (0, 1): g2.at[1], (1, 0): g2.at[2], (1, 1): g2.at[3],
                (2, 0): g2x_in.at[0], (2, 1): g2x_in.at[1], (0, 2): g2y_in.at[0], (1, 2): g2y_in.at[1],
                (2, 2): g2c_in.at[0]}
    for a in range(3):
        for b in range(3):
            total = 0.0
            for from_x, dx in reads[a]:
                for from_y, dy in reads[b]:
                    at, tap = sources[from_x, from_y] * 16, (dx * 3 + dy) * 256
                    total = total + back[at:at + 16, tap:tap + 256]
            value = slope_at[a, b][...] * (total[:, 0:128] + up(total[:, 128:256]))
            d2s[a * 3 + b, pl.ds(0, 16, stride=2), :] = value[:, 0:64]
            d2s[a * 3 + b, pl.ds(1, 16, stride=2), :] = value[:, 64:128]

    delta = jnp.concatenate([d2s[a * 3 + b].astype(LOW) for a, b in OWN], axis=0)
    grad = dot(lhs2t[...], delta)

    def second_block(block):
        if block > 26:
            return jnp.zeros((64, 64), WIDE)
        start = (block // 3) * 256 + (192, 0, 64)[block % 3]
        return grad[start:start + 64]

    for block in range(14):
        both = jnp.concatenate([second_block(block), second_block(block + 14)], axis=1)
        grads_b[block * 4:(block + 1) * 4] = both.reshape(4, ROWS, LANES)

    sums = {}
    for dx in range(3):
        for dy in range(3):
            cells = [((1 if dx == 0 else 0) + a, (1 if dy == 0 else 0) + b) for a, b in OWN]
            stacked = jnp.concatenate([d2s[a * 3 + b].astype(LOW) for a, b in cells], axis=0)
            tap = (dx * 3 + dy) * 256
            back = dot(stacked, second[tap:tap + 256], transposed=True)
            for index, (a, b) in enumerate(cells):
                place = (2 * a + dx - 1, 2 * b + dy - 1)
                part = back[index * 32:(index + 1) * 32]
                sums[place] = sums[place] + part if place in sums else part
    for a in range(4):
        for b in range(4):
            total = sums[a, b]
            value = g1[b, a * 32:(a + 1) * 32] * (total[:, 0:128] + up(total[:, 128:256]))
            d1[b * 128 + a * 32:b * 128 + (a + 1) * 32, :] = value.astype(LOW)
    grad = dot(c1t[...], d1[...])
    for dz in range(3):
        start = (0, SLOT, 2 * SLOT)[dz]
        other = (2 * SLOT, 128, 128 + SLOT)[dz]
        w1c[dz * SLOT:(dz + 1) * SLOT, :] = jnp.concatenate(
            [grad[start:start + SLOT, 0:64] + grad[other:other + SLOT, 64:128], jnp.zeros((SLOT, 64), WIDE)], axis=1)
    w1c[120:128, :] = jnp.zeros((8, 128), WIDE)
    grads_b[SECOND_UNITS:SECOND_UNITS + FIRST_UNITS] = w1c[0:128, :].reshape(FIRST_UNITS, ROWS, LANES)

    small.start_swap()
    large.start_depth()
    small.start_plane()
    large.start_final()
    small.start_depth()
    large.start_gather()
    small.start_final()
    large.pass_on()
    small.start_gather()
    small.pass_on()
    total = large.finish()
    for lanes in range(2):
        out3[:, lanes * 128:(lanes + 1) * 128] = total[lanes * 108:(lanes + 1) * 108].reshape(1728, LANES)
    total = small.finish()
    both = total[0:SECOND_UNITS].reshape(896, LANES)
    out2[0:896, :] = both[:, 0:64]
    out2[896:1728, :] = both[0:832, 64:128]
    w1c[0:128, :] = total[SECOND_UNITS:SECOND_UNITS + FIRST_UNITS].reshape(128, LANES).astype(WIDE)
    for dx in range(3):
        for dy in range(3):
            for dz in range(3):
                out1[dx, dy, dz] = w1c[pl.ds(dz * SLOT + (dx * 3 + dy) * 4, 4), 0:64]
    volumes.sent()
    slopes.sent()
    deltas.sent()


def local(sizes, volume, cotangent, first_weight, second_weight, third_weight):
    dp, size_x, size_y = sizes
    plane = min(4, size_y // CORES) * dp
    depth = size_x * (size_y // (CORES * min(4, size_y // CORES)))
    grain = CORES * plane
    units_a = -(-THIRD_UNITS // grain) * grain
    units_b = -(-(FIRST_UNITS + SECOND_UNITS) // grain) * grain
    kept = cotangent.shape[1]
    spread = size_x * kept * ROWS
    vmem, sems = pltpu.VMEM, pltpu.SemaphoreType.DMA
    block = volume.shape[1:]
    whole, anywhere = pl.BlockSpec(memory_space=pltpu.VMEM), pl.BlockSpec(memory_space=pl.ANY)
    grads = pl.pallas_call(
        functools.partial(kernel, sizes),
        out_shape=(
            jax.ShapeDtypeStruct((3, 3, 3, 4, 64), WIDE),
            jax.ShapeDtypeStruct((1728, 64), LOW),
            jax.ShapeDtypeStruct((1728, 256), LOW),
        ),
        in_specs=[whole, whole, whole, anywhere, anywhere, anywhere],
        out_specs=(whole, whole, whole),
        scratch_shapes=[
            vmem(block, LOW), vmem(block, LOW), vmem(block, LOW),
            vmem((256, 128), WIDE), vmem((3, 3, 4, 64, 64), LOW), vmem((3, 3, 4, 64, 256), LOW), vmem((768, 896), LOW),
            sems((5,)), sems((2, 9)),
            vmem((size_x, kept, size_y, ROWS), LOW), sems((2, size_x)),
            vmem((size_y, 8, spread), WIDE), vmem((size_y, 8, spread), WIDE), sems((2, size_y)),
            vmem((8, 136, 128), WIDE), vmem((5, 256, 128), LOW), vmem((7, 224, 256), LOW), vmem((4, 128, 128), WIDE),
            vmem((7, 224, 128), LOW), vmem((7, 224, 128), LOW), vmem((288, 2304), LOW), vmem((288, 64), WIDE),
            vmem((4, 16, 128), WIDE), vmem((2, 16, 128), WIDE),
            vmem((2, 16, 128), WIDE), vmem((2, 16, 128), WIDE), vmem((1, 16, 128), WIDE),
            vmem((16, 2304), WIDE), vmem((16, 256), LOW), vmem((16, 256), LOW), vmem((16, 256), LOW), vmem((16, 256), LOW),
            vmem((2304, 128), LOW), vmem((256, 512), LOW), vmem((9, 32, 64), WIDE), vmem((512, 128), LOW),
            vmem((units_a, ROWS, LANES), WIDE), vmem((units_b, ROWS, LANES), WIDE),
            *Reduction.scratch(units_a, plane, depth), *Reduction.scratch(units_b, plane, depth),
        ],
        compiler_params=pltpu.CompilerParams(collective_id=1, has_side_effects=True, vmem_limit_bytes=48 * 2**20),
        cost_estimate=pl.CostEstimate(flops=1_000_000_000, bytes_accessed=8_000_000, transcendentals=1_000_000),
    )(volume[0], cotangent[0], first_weight, second_weight, third_weight, jnp.asarray(selection(), LOW))
    return (
        grads[0],
        grads[1].astype(WIDE).reshape(3, 3, 3, 64, 64),
        grads[2].astype(WIDE).reshape(3, 3, 3, 64, 256),
    )


def solution(mesh):
    sizes = tuple(mesh.shape[name] for name in ("dp", "sx", "sy"))
    placed = (P("dp", None, "sx", "sy", None), P("dp", ("sx", "sy"), None, None, None), P(), P(), P())
    return jax.shard_map(
        functools.partial(local, sizes), mesh=mesh, in_specs=placed, out_specs=(P(), P(), P()), check_vma=False)
```

time: 874 us -> 94.5 us (0.11)
  waiting for transfers between devices: 371 us -> 0 us
  local copies, waits for them, and re-layouts: 226 us -> 6.56 us
  blocking collectives: 121 us -> 0 us
  Pallas kernels: 0 us -> 84.5 us
  matrix products: 67.3 us -> 0 us
  starting transfers between devices: 64.6 us -> 0 us
  between operations: 15.2 us -> 0.65 us
    psum x1 -> x0, waiting for transfers between devices: 362 us -> none  [local(): return lax.psum((grad_first, grad_second, grad_third), ('dp', 'sx', 'sy'))]
    slice x67 -> x0, local copies, waits for them, and re-layouts: 200 us -> none  [the longest x56 197 us: kernel_grad(): lax.slice(padded, (0, 0, shift_x, shift_y, shift_z), (samples, channels_i...]
    psum x1 -> x0, blocking collectives: 121 us -> none  [local(): return lax.psum((grad_first, grad_second, grad_third), ('dp', 'sx', 'sy'))]
    pallas_call x0 -> x1, Pallas kernels: none -> 84.5 us  [local(): pl.pallas_call(functools.partial(kernel, sizes), out_shape=(jax.ShapeDtyp...]
    dot_general x81 -> x0, matrix products: 58 us -> none  [kernel_grad(): jnp.einsum('bcxyz,boxyz->co', window, delta, preferred_element_type=jnp.f...]
    all_to_all x1 -> x0, starting transfers between devices: 33.2 us -> none  [to_blocks(): lax.all_to_all(pieces, ('sx', 'sy'), split_axis=0, concat_axis=2, tiled=T...]
    ppermute x10 -> x0, starting transfers between devices: 31.3 us -> none  [passed_along(): lax.ppermute(value, axis, [(source, source + steps) for source in range(l...]
    conv_general_dilated x5 -> x0, matrix products: 9.25 us -> none  [the longest x3 6.86 us: convolve(): lax.conv_general_dilated(field, kernel, (2, 2, 2), margins, dimension_num...]
  transfers between devices with their start and end apart: 12 -> 0, of which waited for: 7 -> 0; matrix products, arithmetic and copies ran while one was open for 31% -> 0% of each run, Pallas kernels for 0% -> 0%
where the time goes in v1:
time: 94.5 us; the launch traced here: 94.1 us
  Pallas kernels  84.5 us (89%)
  local copies, waits for them, and re-layouts  6.56 us (7%)
  other arithmetic  2.42 us (3%)
    pallas_call x1, Pallas kernels, local(): pl.pallas_call(functools.partial(kernel, sizes), out_shape=(jax.ShapeDtyp...  84.5 us
    unnamed x13, local copies, waits for them, and re-layouts  6.56 us

profile of v1, /device:TPU:1, one launch (start us, length us, event | category | flops | bytes accessed | tf_op | source)
XLA Modules:
  0.0 94.1 jit_solution(3152395663943561675)
XLA Ops:
  0.6 0.0 copy-start
  0.6 1.2 %copy-done = bf16[3,3,3,64,256]{4,3,2,1,0:T(8,128)(2,1)S(1)} copy-done((bf16[3,3,3,64,256]{4,3,2,1,0:T(8,128)(2,1)S(1)}, bf16[3,3,3,64,256]{4,3,2,1,0:T(8,128)(2,1)}, u32[]{:S(2)}) %copy-start) | copy-done | bytes 884760
  1.8 0.0 copy-start.1
  1.8 1.0 %copy-done.1 = bf16[3,3,3,64,64]{4,3,2,1,0:T(8,128)(2,1)S(1)} copy-done((bf16[3,3,3,64,64]{4,3,2,1,0:T(8,128)(2,1)S(1)}, bf16[3,3,3,64,64]{4,3,2,1,0:T(8,128)(2,1)}, u32[]{:S(2)}) %copy-start.1) | copy-done | bytes 221208
  2.8 0.0 copy-start.2
  2.8 0.8 copy-done.2
  3.7 0.0 copy-start.3
  3.7 0.8 copy-done.3
  4.5 0.0 copy-start.4
  4.5 0.7 copy-done.4
  5.2 0.0 copy-start.5
  5.2 1.3 %copy-done.5 = bf16[768,896]{1,0:T(8,128)(2,1)S(1)} copy-done((bf16[768,896]{1,0:T(8,128)(2,1)S(1)}, bf16[768,896]{1,0:T(8,128)(2,1)}, u32[]{:S(2)}) %copy-start.5) | copy-done | bytes 1376280
  6.6 84.5 %shard_map.85 = (f32[3,3,3,4,64]{4,3,2,1,0:T(4,128)S(1)}, bf16[1728,64]{1,0:T(8,128)(2,1)S(1)}, bf16[1728,256]{1,0:T(8,128)(2,1)S(1)}) custom-call(bf16[4,8,8,128]{3,2,1,0:T(8,128)(2,1)S(1)} %bitcast.8, bf16[2,8,16,16]{3,2,1,0:T(8,128)(2,1)S(1)} %bitcast.9, bf16[3,3,3,4,64]{4,3,2,1,0:T(4,128)(2,1)S(1)} %copy-done.4, ...), custom_call_target="tpu_custom_call" | custom-call | flops 1000000000 | bytes 8000000 | tf_op jit(solution)/shard_map/pallas_call | solution.py:538
  91.0 1.4 %convert.3 = f32[3,3,3,64,256]{4,3,2,1,0:T(8,128)} convert(bf16[3,3,3,64,256]{4,3,2,1,0:T(8,128)(2,1)S(1)} %bitcast.6) | non-fusion elementwise | flops 442368 | bytes 2654208 | tf_op jit(solution)/shard_map/reshape | solution.py:568
  92.4 1.0 %convert.2 = f32[3,3,3,64,64]{4,3,2,1,0:T(8,128)} convert(bf16[3,3,3,64,64]{4,3,2,1,0:T(8,128)(2,1)S(1)} %bitcast.7) | non-fusion elementwise | flops 110592 | bytes 663552 | tf_op jit(solution)/shard_map/reshape | solution.py:567
  93.5 0.6 copy.10
Async XLA Ops:
  0.6 1.2 %copy-start = (bf16[3,3,3,64,256]{4,3,2,1,0:T(8,128)(2,1)S(1)}, bf16[3,3,3,64,256]{4,3,2,1,0:T(8,128)(2,1)}, u32[]{:S(2)}) copy-start(bf16[3,3,3,64,256]{4,3,2,1,0:T(8,128)(2,1)} %w3.1) | copy-start | bytes 2654212
  1.8 1.0 %copy-start.1 = (bf16[3,3,3,64,64]{4,3,2,1,0:T(8,128)(2,1)S(1)}, bf16[3,3,3,64,64]{4,3,2,1,0:T(8,128)(2,1)}, u32[]{:S(2)}) copy-start(bf16[3,3,3,64,64]{4,3,2,1,0:T(8,128)(2,1)} %w2.1) | copy-start | bytes 663556
  2.8 0.8 copy-start.2
  3.7 0.8 copy-start.3
  4.5 0.7 copy-start.4
  5.2 1.3 %copy-start.5 = (bf16[768,896]{1,0:T(8,128)(2,1)S(1)}, bf16[768,896]{1,0:T(8,128)(2,1)}, u32[]{:S(2)}) copy-start(bf16[768,896]{1,0:T(8,128)(2,1)} %constant.2.clone.select) | copy-start | bytes 4128772

commit v2 on v1

--- a/solution.py
+++ b/solution.py
@@ -69,7 +69,9 @@
         self.y, self.sx, self.sy = (lax.axis_index(name) for name in ("dp", "sx", "sy"))
         self.core = lax.rem(self.sy, CORES)
         self.p = lax.rem(self.sy // CORES, self.chips_x) * dp + self.y
-        self.z = (self.sy // (CORES * self.chips_x)) * sx + self.sx
+        self.mixed = CORES * self.chips_x
+        self.t = lax.rem(self.sy, self.mixed)
+        self.z = (self.sy // self.mixed) * sx + self.sx
 
     def device(self, core=None, p=None, z=None):
         core = self.core if core is None else core
@@ -95,8 +97,8 @@
 
 
 class Reduction:
-    def __init__(self, here, grads, refs):
-        self.here, self.grads = here, grads
+    def __init__(self, here, grads, refs, direct):
+        self.here, self.grads, self.direct = here, grads, direct
         (self.half_out, self.half_in, self.plane_out, self.plane_in, self.depth_out, self.depth_in,
          self.final, self.gathered, self.half_sems, self.plane_sems, self.depth_sems, self.final_sems,
          self.gather_sems, self.pair_sems) = refs
@@ -104,12 +106,12 @@
         self.half = here.plane * self.share
         self.partner = here.device(core=1 - here.core)
         owners = [unit * here.depth // self.share for unit in range(self.share)]
-        self.owned = [(unit, owner, unit - owners.index(owner)) for unit, owner in enumerate(owners)]
+        self.owned = [] if direct else [(unit, owner, unit - owners.index(owner)) for unit, owner in enumerate(owners)]
 
     @staticmethod
-    def scratch(units, plane, depth):
+    def scratch(units, plane, depth, direct):
         share = units // (CORES * plane)
-        slots = -(-share // depth)
+        slots = share if direct else -(-share // depth)
         unit = (ROWS, LANES)
         return [
             pltpu.VMEM((plane * share, *unit), LOW),
@@ -117,7 +119,7 @@
             pltpu.VMEM((plane, share, *unit), LOW),
             pltpu.VMEM((plane, share, *unit), LOW),
             pltpu.VMEM((share, *unit), LOW),
-            pltpu.VMEM((slots, depth, *unit), LOW),
+            pltpu.VMEM((depth, slots, *unit) if direct else (slots, depth, *unit), LOW),
             pltpu.VMEM((share, *unit), LOW),
             pltpu.VMEM((CORES, plane, share, *unit), LOW),
             pltpu.SemaphoreType.DMA((2, 1)),
@@ -156,10 +158,17 @@
         self.plane_in[here.p] = self.plane_out[here.p]
         others(here.plane, here.p, lambda q: self.to_plane(q, q).wait())
         self.depth_out[...] = jnp.sum(self.plane_in[...].astype(WIDE), axis=0).astype(LOW)
+        if self.direct:
+            others(here.depth, here.z, lambda q: self.to_all(q, here.z).start())
+            return
         for unit, owner, slot in self.owned:
             @pl.when(here.z != owner)
             def _():
                 self.to_depth(unit, owner, slot, here.z).start()
+
+    def to_all(self, q, source_slot):
+        here = self.here
+        return copy(self.depth_out, self.depth_in.at[source_slot], self.depth_sems, q, source_slot, here.device(z=q))
 
     def to_final(self, unit, slot, q):
         here = self.here
@@ -184,6 +193,10 @@
 
     def start_gather(self):
         here = self.here
+        if self.direct:
+            self.depth_in[here.z] = self.depth_out[...]
+            others(here.depth, here.z, lambda q: self.to_all(q, q).wait())
+            self.final[...] = jnp.sum(self.depth_in[...].astype(WIDE), axis=0).astype(LOW)
         for unit, owner, slot in self.owned:
             @pl.when(here.z != owner)
             def _():
@@ -259,56 +272,58 @@
                 move.wait_send()
 
 
-def kernel(sizes, volume, cotangent, w1, w2, w3, select, out1, out2, out3,
-           vx, vy, vc, w1c, w2s, w3s, sel, local_sems, halo_sems, r1, r1_sems, s2, r2, r2_sems,
+def kernel(sizes, volume_hbm, cotangent_hbm, w1_hbm, w2, w3, select, out1, out2, out3,
+           volume, vx, vy, vc, cotangent, w1, w1c, w2s, w3s, sel, local_sems, halo_sems, s1, r1, r1_sems, s2, r2, r2_sems,
            dts, xoff, c1, g1, act1, act1s, lhs2, pre2, g2, g2y, g2x_in, g2y_in, g2c_in, lhs3, d3, d3x, d3y, d3c,
            lhs2t, c1t, d2s, d1, grads_a, grads_b, *reductions):
     here = Place(*sizes)
     _, size_x, size_y = sizes
-    kept = cotangent.shape[0]
+    mixed, depth = here.mixed, here.depth
+    kept, high = cotangent.shape[0], size_y // mixed
+
+    barrier = pltpu.get_barrier_semaphore()
+
+    def greet(device):
+        pl.semaphore_signal(barrier, inc=1, device_id=device, device_id_type=MESH)
+
+    def at_mixed(t):
+        return (here.y, here.sx, here.sy - here.t + t)
+
+    others(depth, here.z, lambda q: greet(here.device(z=q)))
+    others(mixed, here.t, lambda q: greet(at_mixed(q)))
+    others(here.plane, here.p, lambda q: greet(here.device(p=q)))
+    expected = depth + mixed + here.plane - 3
+    for along_x in range(2):
+        for step in (-1, 1):
+            inside = here.sy > 0 if step < 0 else here.sy < size_y - 1
+            if along_x:
+                inside = jnp.logical_and(inside, here.sx > 0 if step < 0 else here.sx < size_x - 1)
+            expected = expected + inside.astype(jnp.int32)
+
+            @pl.when(inside)
+            def _():
+                greet((here.y, here.sx + step * along_x, here.sy + step))
 
     loads = [
-        pltpu.make_async_copy(select, sel, local_sems.at[0]),
-        pltpu.make_async_copy(w2.at[:, :, pl.ds(1, 2)], w2s.at[:, :, pl.ds(0, 2)], local_sems.at[1]),
-        pltpu.make_async_copy(w2.at[:, :, pl.ds(0, 1)], w2s.at[:, :, pl.ds(3, 1)], local_sems.at[2]),
-        pltpu.make_async_copy(w3.at[:, :, pl.ds(1, 2)], w3s.at[:, :, pl.ds(0, 2)], local_sems.at[3]),
-        pltpu.make_async_copy(w3.at[:, :, pl.ds(0, 1)], w3s.at[:, :, pl.ds(3, 1)], local_sems.at[4]),
+        pltpu.make_async_copy(w1_hbm, w1, local_sems.at[0]),
+        pltpu.make_async_copy(cotangent_hbm, cotangent, local_sems.at[1]),
+        pltpu.make_async_copy(volume_hbm, volume, local_sems.at[2]),
+        pltpu.make_async_copy(select, sel, local_sems.at[3]),
+        pltpu.make_async_copy(w2.at[:, :, pl.ds(1, 2)], w2s.at[:, :, pl.ds(0, 2)], local_sems.at[4]),
+        pltpu.make_async_copy(w2.at[:, :, pl.ds(0, 1)], w2s.at[:, :, pl.ds(3, 1)], local_sems.at[5]),
+        pltpu.make_async_copy(w3.at[:, :, pl.ds(1, 2)], w3s.at[:, :, pl.ds(0, 2)], local_sems.at[6]),
+        pltpu.make_async_copy(w3.at[:, :, pl.ds(0, 1)], w3s.at[:, :, pl.ds(3, 1)], local_sems.at[7]),
     ]
     for load in loads:
         load.start()
-
-    barrier = pltpu.get_barrier_semaphore()
-
-    def greet(device):
-        pl.semaphore_signal(barrier, inc=1, device_id=device, device_id_type=MESH)
-
-    lower = jnp.logical_and(here.sx > 0, here.sy > 0)
-    upper = jnp.logical_and(here.sx < size_x - 1, here.sy < size_y - 1)
-    others(here.depth, here.z, lambda q: greet(here.device(z=q)))
-    others(size_y, here.sy, lambda q: greet((here.y, here.sx, q)))
-    others(here.plane, here.p, lambda q: greet(here.device(p=q)))
-
-    @pl.when(lower)
-    def _():
-        greet((here.y, here.sx - 1, here.sy - 1))
-
-    @pl.when(upper)
-    def _():
-        greet((here.y, here.sx + 1, here.sy + 1))
-
-    pl.semaphore_wait(barrier, here.depth + size_y + here.plane - 3 + lower.astype(jnp.int32) + upper.astype(jnp.int32))
-
-    volumes = Halo(here, sizes, 1, halo_sems, 0, ((1, 0, volume, vx), (0, 1, volume, vy), (1, 1, volume, vc)))
-    volumes.start()
-
-    def to_rows(q, source_slot):
-        return copy(cotangent.at[:, q], r1.at[source_slot], r1_sems, q, source_slot, (here.y, q, here.sy))
-
-    others(size_x, here.sx, lambda q: to_rows(q, here.sx).start())
-    r1[here.sx] = cotangent[:, here.sx]
-
+    for ref in (w2s, w3s):
+        ref[:, :, 2] = jnp.zeros((3, 3, *ref.shape[3:]), LOW)
+    for index in range(8):
+        dts[index, 0:8, :] = jnp.zeros((8, 128), WIDE)
     w1c[...] = jnp.zeros(w1c.shape, WIDE)
     blank = jnp.zeros((4, 64), WIDE)
+
+    loads[0].wait()
     for offset in range(5):
         base = offset * SLOT if offset < 3 else 128 + (offset - 3) * SLOT
         for dx in range(3):
@@ -316,40 +331,55 @@
                 left = w1[dx, dy, offset].astype(WIDE) if offset <= 2 else blank
                 right = w1[dx, dy, offset - 2].astype(WIDE) if offset >= 2 else blank
                 w1c[pl.ds(base + (dx * 3 + dy) * 4, 4), :] = jnp.concatenate([left, right], axis=1)
-    for ref in (w2s, w3s):
-        ref[:, :, 2] = jnp.zeros((3, 3, *ref.shape[3:]), LOW)
-    for index in range(8):
-        dts[index, 0:8, :] = jnp.zeros((8, 128), WIDE)
-
-    others(size_x, here.sx, lambda q: to_rows(q, q).wait())
-    groups = size_x * kept
-    spread = groups * ROWS
+
+    loads[1].wait()
+    spread = size_x * kept * ROWS
     lane = lax.broadcasted_iota(jnp.int32, (ROWS, spread), 1)
     row = lax.broadcasted_iota(jnp.int32, (ROWS, spread), 0)
     repeat = jnp.where((lane & (ROWS - 1)) == row, 1.0, 0.0).astype(LOW)
-    wide = dot(r1[...].reshape(groups * size_y, ROWS), repeat).reshape(groups, size_y, spread)
+    wide = dot(cotangent[...].reshape(kept * size_x * size_y, ROWS), repeat).reshape(kept * size_x, size_y, spread)
     lane = lax.broadcasted_iota(jnp.int32, wide.shape, 2)
     group = lax.broadcasted_iota(jnp.int32, wide.shape, 0)
-    strips = jnp.sum(jnp.where((lane >> 4) == group, wide, 0.0), axis=0)
-    s2[...] = jnp.broadcast_to(strips[:, None, :], s2.shape)
+    strips = jnp.sum(jnp.where((lane >> 4) == lax.rem(group, size_x) * kept + group // size_x, wide, 0.0), axis=0)
+    rows = 8 // high
+    for t in range(mixed):
+        for part in range(high):
+            y = part * mixed + t
+            s1[t, part * rows:(part + 1) * rows, :] = jnp.broadcast_to(strips[y:y + 1, :], (rows, spread))
+
+    pl.semaphore_wait(barrier, expected)
+    volumes = Halo(here, sizes, 1, halo_sems, 0, (
+        (1, 0, volume_hbm, vx), (0, 1, volume_hbm, vy), (1, 1, volume_hbm, vc)))
+    volumes.start()
+
+    def to_mixed(q, source_slot):
+        return copy(s1.at[q], r1.at[source_slot], r1_sems, q, source_slot, at_mixed(q))
 
     def to_cell(q, source_slot):
-        return copy(s2.at[q], r2.at[source_slot], r2_sems, q, source_slot, (here.y, here.sx, q))
-
-    others(size_y, here.sy, lambda q: to_cell(q, here.sy).start())
-    r2[here.sy] = s2[here.sy]
-
-    loads[0].wait()
+        return copy(s2.at[q], r2.at[source_slot], r2_sems, q, source_slot, here.device(z=q))
+
+    others(mixed, here.t, lambda q: to_mixed(q, here.t).start())
+    r1[here.t] = s1[here.t]
+    others(mixed, here.t, lambda q: to_mixed(q, q).wait())
+    for part in range(high):
+        strips = jnp.max(r1[:, part * rows:(part + 1) * rows, :], axis=1)
+        for x in range(size_x):
+            s2[part * size_x + x] = strips[:, x * kept * ROWS:(x + 1) * kept * ROWS]
+    others(depth, here.z, lambda q: to_cell(q, here.z).start())
+    r2[here.z] = s2[here.z]
+
+    for load in loads[2:4]:
+        load.wait()
     volumes.wait()
 
     for pair in range(8):
         before, inside = (vc, vx) if pair < 4 else (vy, volume)
         tiles = []
-        for odd in range(2):
-            x = (2 * pair + odd) % 8
-            for channel in range(4):
-                tiles += [before[channel, x].astype(WIDE), inside[channel, x].astype(WIDE)]
-        dts[pair, 8:136, :] = jnp.concatenate(tiles, axis=0).T
+        for channel in range(4):
+            at = channel * 64 + (pair % 4) * 16
+            tiles.append([ref[at:at + 16, :].astype(WIDE) for ref in (before, inside)])
+        ordered = [both[odd * 8:(odd + 1) * 8] for odd in range(2) for refs in tiles for both in refs]
+        dts[pair, 8:136, :] = jnp.concatenate(ordered, axis=0).T
     for offset in range(5):
         for pair in range(8):
             xoff[offset, pair * 32:(pair + 1) * 32, :] = dts[pair, pl.ds(7 + offset, 32, stride=4), :].astype(LOW)
@@ -376,7 +406,7 @@
                 rows = slice((2 * x + dx) * 32, (2 * x + dx + 1) * 32)
                 lhs2[index * 32:(index + 1) * 32, at:at + 128] = act1[2 * y + dy, rows, :]
                 lhs2[index * 32:(index + 1) * 32, at + 128:at + 256] = act1s[2 * y + dy, rows, :]
-    for load in loads[1:3]:
+    for load in loads[4:6]:
         load.wait()
     second = w2s[...].reshape(2304, 64)
     pre2[...] = dot(lhs2[...], second)
@@ -396,17 +426,17 @@
         (1, 0, g2.at[pl.ds(0, 2)], g2x_in), (0, 1, g2y, g2y_in), (1, 1, g2.at[pl.ds(0, 1)], g2c_in)))
     slopes.start()
 
-    others(size_y, here.sy, lambda q: to_cell(q, q).wait())
-    strips = jnp.max(r2[...], axis=1).T.astype(LOW)
-    channel = lax.broadcasted_iota(jnp.int32, (size_y, 256), 1)
-    owner = lax.broadcasted_iota(jnp.int32, (size_y, 256), 0)
-    choose = jnp.where(lax.rem(channel // kept, size_y) == owner, 1.0, 0.0).astype(LOW)
-    wide = dot(strips, choose).reshape(groups, ROWS, 256)
-    channel = lax.broadcasted_iota(jnp.int32, wide.shape, 2)
-    group = lax.broadcasted_iota(jnp.int32, wide.shape, 0)
-    mine = (channel // (kept * size_y)) * kept + lax.rem(channel, kept) == group
-    upstream = jnp.sum(jnp.where(mine, wide, 0.0), axis=0)
-    for load in loads[3:5]:
+    others(depth, here.z, lambda q: to_cell(q, q).wait())
+    strips = r2[...].reshape(depth * mixed, kept * ROWS).T.astype(LOW)
+    sender = lax.broadcasted_iota(jnp.int32, (depth * mixed, 256), 0)
+    channel = lax.broadcasted_iota(jnp.int32, (depth * mixed, 256), 1)
+    z, t = sender // mixed, lax.rem(sender, mixed)
+    channel = channel - ((lax.rem(z, size_x) * size_y + (z // size_x) * mixed + t) * kept)
+    upstream = 0.0
+    for k in range(kept):
+        choose = jnp.where(channel == k, 1.0, 0.0).astype(LOW)
+        upstream = upstream + dot(strips[k * ROWS:(k + 1) * ROWS], choose)
+    for load in loads[6:8]:
         load.wait()
     third = w3s[...].reshape(2304, 256)
     pre = dot(lhs3[...].astype(LOW), third)
@@ -426,8 +456,8 @@
     if spare:
         grads_a[THIRD_UNITS:] = jnp.zeros((spare, ROWS, LANES), WIDE)
     many = len(reductions) // 2
-    large = Reduction(here, grads_a, reductions[:many])
-    small = Reduction(here, grads_b, reductions[many:])
+    large = Reduction(here, grads_a, reductions[:many], False)
+    small = Reduction(here, grads_b, reductions[many:], True)
     large.start_swap()
 
     for block in range(18):
@@ -499,12 +529,11 @@
     small.start_swap()
     large.start_depth()
     small.start_plane()
+    small.start_depth()
     large.start_final()
-    small.start_depth()
     large.start_gather()
-    small.start_final()
+    small.start_gather()
     large.pass_on()
-    small.start_gather()
     small.pass_on()
     total = large.finish()
     for lanes in range(2):
@@ -533,23 +562,23 @@
     kept = cotangent.shape[1]
     spread = size_x * kept * ROWS
     vmem, sems = pltpu.VMEM, pltpu.SemaphoreType.DMA
-    block = volume.shape[1:]
-    whole, anywhere = pl.BlockSpec(memory_space=pltpu.VMEM), pl.BlockSpec(memory_space=pl.ANY)
+    mixed = CORES * min(4, size_y // CORES)
+    whole, far = pl.BlockSpec(memory_space=pltpu.VMEM), pl.BlockSpec(memory_space=pltpu.HBM)
     grads = pl.pallas_call(
         functools.partial(kernel, sizes),
         out_shape=(
-            jax.ShapeDtypeStruct((3, 3, 3, 4, 64), WIDE),
-            jax.ShapeDtypeStruct((1728, 64), LOW),
-            jax.ShapeDtypeStruct((1728, 256), LOW),
+            pltpu.VMEM((3, 3, 3, 4, 64), WIDE),
+            pltpu.VMEM((1728, 64), LOW),
+            pltpu.VMEM((1728, 256), LOW),
         ),
-        in_specs=[whole, whole, whole, anywhere, anywhere, anywhere],
+        in_specs=[far] * 6,
         out_specs=(whole, whole, whole),
         scratch_shapes=[
-            vmem(block, LOW), vmem(block, LOW), vmem(block, LOW),
-            vmem((256, 128), WIDE), vmem((3, 3, 4, 64, 64), LOW), vmem((3, 3, 4, 64, 256), LOW), vmem((768, 896), LOW),
-            sems((5,)), sems((2, 9)),
-            vmem((size_x, kept, size_y, ROWS), LOW), sems((2, size_x)),
-            vmem((size_y, 8, spread), WIDE), vmem((size_y, 8, spread), WIDE), sems((2, size_y)),
+            vmem((256, 128), LOW), vmem((256, 128), LOW), vmem((256, 128), LOW), vmem((256, 128), LOW),
+            vmem(cotangent.shape[1:], LOW), vmem(first_weight.shape, LOW), vmem((256, 128), WIDE), vmem((3, 3, 4, 64, 64), LOW), vmem((3, 3, 4, 64, 256), LOW), vmem((768, 896), LOW),
+            sems((8,)), sems((2, 9)),
+            vmem((mixed, 8, spread), WIDE), vmem((mixed, 8, spread), WIDE), sems((2, mixed)),
+            vmem((depth, mixed, kept * ROWS), WIDE), vmem((depth, mixed, kept * ROWS), WIDE), sems((2, depth)),
             vmem((8, 136, 128), WIDE), vmem((5, 256, 128), LOW), vmem((7, 224, 256), LOW), vmem((4, 128, 128), WIDE),
             vmem((7, 224, 128), LOW), vmem((7, 224, 128), LOW), vmem((288, 2304), LOW), vmem((288, 64), WIDE),
             vmem((4, 16, 128), WIDE), vmem((2, 16, 128), WIDE),
@@ -557,11 +586,11 @@
             vmem((16, 2304), WIDE), vmem((16, 256), LOW), vmem((16, 256), LOW), vmem((16, 256), LOW), vmem((16, 256), LOW),
             vmem((2304, 128), LOW), vmem((256, 512), LOW), vmem((9, 32, 64), WIDE), vmem((512, 128), LOW),
             vmem((units_a, ROWS, LANES), WIDE), vmem((units_b, ROWS, LANES), WIDE),
-            *Reduction.scratch(units_a, plane, depth), *Reduction.scratch(units_b, plane, depth),
+            *Reduction.scratch(units_a, plane, depth, False), *Reduction.scratch(units_b, plane, depth, True),
         ],
-        compiler_params=pltpu.CompilerParams(collective_id=1, has_side_effects=True, vmem_limit_bytes=48 * 2**20),
+        compiler_params=pltpu.CompilerParams(collective_id=1, has_side_effects=True, vmem_limit_bytes=60 * 2**20),
         cost_estimate=pl.CostEstimate(flops=1_000_000_000, bytes_accessed=8_000_000, transcendentals=1_000_000),
-    )(volume[0], cotangent[0], first_weight, second_weight, third_weight, jnp.asarray(selection(), LOW))
+    )(volume.reshape(256, 128), cotangent[0], first_weight, second_weight, third_weight, jnp.asarray(selection(), LOW))
     return (
         grads[0],
         grads[1].astype(WIDE).reshape(3, 3, 3, 64, 64),

time: 94.5 us -> 79.5 us (0.84)
  Pallas kernels: 84.5 us -> 75.3 us
  local copies, waits for them, and re-layouts: 6.56 us -> 0.62 us
    pallas_call x1, Pallas kernels: 84.5 us -> 75.3 us  [local(): pl.pallas_call(functools.partial(kernel, sizes), out_shape=(pltpu.VMEM((3...]
    unnamed x13 -> x1, local copies, waits for them, and re-layouts: 6.56 us -> 0.62 us
where the time goes in v2:
time: 79.5 us; the launch traced here: 79 us
  Pallas kernels  75.3 us (95%)
  other arithmetic  2.42 us (3%)
    pallas_call x1, Pallas kernels, local(): pl.pallas_call(functools.partial(kernel, sizes), out_shape=(pltpu.VMEM((3...  75.3 us

profile of v2, /device:TPU:1, one launch (start us, length us, event | category | flops | bytes accessed | tf_op | source)
XLA Modules:
  0.0 79.0 jit_solution(8917862117775277724)
XLA Ops:
  0.6 75.3 %shard_map.85 = (f32[3,3,3,4,64]{4,3,2,1,0:T(4,128)S(1)}, bf16[1728,64]{1,0:T(8,128)(2,1)S(1)}, bf16[1728,256]{1,0:T(8,128)(2,1)S(1)}) custom-call(bf16[256,128]{1,0:T(8,128)(2,1)} %bitcast.8, bf16[2,8,16,16]{3,2,1,0:T(8,128)(2,1)} %bitcast.9, bf16[3,3,3,4,64]{4,3,2,1,0:T(4,128)(2,1)} %w1_hbm.1, bf16[3,3,3,64,64]{4,3,2,1,0:T(8,128)(2,1)} %w2.1, ...), custom_call_target="tpu_custom_call" | custom-call | flops 1000000000 | bytes 8000000 | tf_op jit(solution)/shard_map/pallas_call | solution.py:567
  75.9 1.4 %convert.3 = f32[3,3,3,64,256]{4,3,2,1,0:T(8,128)} convert(bf16[3,3,3,64,256]{4,3,2,1,0:T(8,128)(2,1)S(1)} %bitcast.6) | non-fusion elementwise | flops 442368 | bytes 2654208 | tf_op jit(solution)/shard_map/reshape | solution.py:597
  77.3 1.0 %convert.2 = f32[3,3,3,64,64]{4,3,2,1,0:T(8,128)} convert(bf16[3,3,3,64,64]{4,3,2,1,0:T(8,128)(2,1)S(1)} %bitcast.7) | non-fusion elementwise | flops 110592 | bytes 663552 | tf_op jit(solution)/shard_map/reshape | solution.py:596
  78.3 0.6 copy.10

commit v3 on v2

--- a/solution.py
+++ b/solution.py
@@ -64,6 +64,7 @@
     def __init__(self, dp, sx, sy):
         self.chips_x = min(4, sy // CORES)
         self.low_z, self.chips_y = sx, dp
+        self.shift_y, self.shift_z = dp.bit_length() - 1, sx.bit_length() - 1
         self.plane = self.chips_x * dp
         self.depth = sx * (sy // (CORES * self.chips_x))
         self.y, self.sx, self.sy = (lax.axis_index(name) for name in ("dp", "sx", "sy"))
@@ -77,17 +78,14 @@
         core = self.core if core is None else core
         p = self.p if p is None else p
         z = self.z if z is None else z
-        chip_x, y = p // self.chips_y, lax.rem(p, self.chips_y)
-        high, low = z // self.low_z, lax.rem(z, self.low_z)
+        chip_x, y = p >> self.shift_y, p & (self.chips_y - 1)
+        high, low = z >> self.shift_z, z & (self.low_z - 1)
         return (y, low, (high * self.chips_x + chip_x) * CORES + core)
 
 
 def others(count, me, body):
-    def step(distance, carry):
-        body(lax.rem(me + distance, count))
-        return carry
-
-    lax.fori_loop(1, count, step, 0)
+    for distance in sorted(range(1, count), key=lambda step: -min(step, count - step)):
+        body((me + distance) & (count - 1))
 
 
 def copy(source, target, sems, at, there, device):
@@ -225,19 +223,16 @@
 
         others(here.plane, here.p, lambda q: self.to_gather(q, q).wait_send())
 
-        def arrived(q, carry):
+        for q in range(here.plane):
             self.to_pair(1 - here.core, q).wait()
-            return carry
-
-        lax.fori_loop(0, here.plane, arrived, 0)
         return self.gathered[...].reshape(-1, ROWS, LANES)
 
 
 class Halo:
-    def __init__(self, here, sizes, step, sems, first, triples):
+    def __init__(self, here, sizes, step, sems, first, triples, needs=None):
         self.items = []
         for index, (along_x, along_y, source, target) in enumerate(triples):
-            sends = receives = None
+            sends = receives = needs
             for along, place, size in ((along_x, here.sx, sizes[1]), (along_y, here.sy, sizes[2])):
                 if not along:
                     continue
@@ -249,14 +244,14 @@
             move = copy(source, target, sems, first + index, first + index, device)
             self.items.append((sends, receives, move, target))
 
-    def start(self):
-        for sends, _, move, _ in self.items:
+    def start(self, first=0, last=None):
+        for sends, _, move, _ in self.items[first:last]:
             @pl.when(sends)
             def _():
                 move.start()
 
-    def wait(self):
-        for _, receives, move, target in self.items:
+    def wait(self, first=0, last=None):
+        for _, receives, move, target in self.items[first:last]:
             @pl.when(receives)
             def _():
                 move.wait_recv()
@@ -272,9 +267,9 @@
                 move.wait_send()
 
 
-def kernel(sizes, volume_hbm, cotangent_hbm, w1_hbm, w2, w3, select, out1, out2, out3,
+def kernel(sizes, volume_hbm, cotangent_hbm, w1_hbm, w2, w3, select, sum_a, sum_b,
            volume, vx, vy, vc, cotangent, w1, w1c, w2s, w3s, sel, local_sems, halo_sems, s1, r1, r1_sems, s2, r2, r2_sems,
-           dts, xoff, c1, g1, act1, act1s, lhs2, pre2, g2, g2y, g2x_in, g2y_in, g2c_in, lhs3, d3, d3x, d3y, d3c,
+           dts, xoff, c1, g1, act1, act1s, lhs2, pre2, g2, g2x, g2y, g2x_in, g2y_in, g2c_in, lhs3, d3, d3x, d3y, d3c,
            lhs2t, c1t, d2s, d1, grads_a, grads_b, *reductions):
     here = Place(*sizes)
     _, size_x, size_y = sizes
@@ -289,9 +284,6 @@
     def at_mixed(t):
         return (here.y, here.sx, here.sy - here.t + t)
 
-    others(depth, here.z, lambda q: greet(here.device(z=q)))
-    others(mixed, here.t, lambda q: greet(at_mixed(q)))
-    others(here.plane, here.p, lambda q: greet(here.device(p=q)))
     expected = depth + mixed + here.plane - 3
     for along_x in range(2):
         for step in (-1, 1):
@@ -304,6 +296,9 @@
             def _():
                 greet((here.y, here.sx + step * along_x, here.sy + step))
 
+    others(depth, here.z, lambda q: greet(here.device(z=q)))
+    others(mixed, here.t, lambda q: greet(at_mixed(q)))
+    others(here.plane, here.p, lambda q: greet(here.device(p=q)))
     loads = [
         pltpu.make_async_copy(w1_hbm, w1, local_sems.at[0]),
         pltpu.make_async_copy(cotangent_hbm, cotangent, local_sems.at[1]),
@@ -348,8 +343,10 @@
             s1[t, part * rows:(part + 1) * rows, :] = jnp.broadcast_to(strips[y:y + 1, :], (rows, spread))
 
     pl.semaphore_wait(barrier, expected)
+    pieces = [pl.ds(64 * channel, 64) for channel in range(4)]
     volumes = Halo(here, sizes, 1, halo_sems, 0, (
-        (1, 0, volume_hbm, vx), (0, 1, volume_hbm, vy), (1, 1, volume_hbm, vc)))
+        *((0, 1, volume_hbm.at[piece], vy.at[piece]) for piece in pieces), (1, 0, volume_hbm, vx)))
+    corners = Halo(here, sizes, 1, halo_sems, 5, [(1, 0, vy.at[piece], vc.at[piece]) for piece in pieces], here.sy > 0)
     volumes.start()
 
     def to_mixed(q, source_slot):
@@ -368,9 +365,13 @@
     others(depth, here.z, lambda q: to_cell(q, here.z).start())
     r2[here.z] = s2[here.z]
 
+    for part in range(4):
+        volumes.wait(part, part + 1)
+        corners.start(part, part + 1)
     for load in loads[2:4]:
         load.wait()
-    volumes.wait()
+    volumes.wait(4)
+    corners.wait()
 
     for pair in range(8):
         before, inside = (vc, vx) if pair < 4 else (vy, volume)
@@ -416,14 +417,16 @@
         if index < 4:
             slope = gelu_slope(pre)
             g2[index] = slope
+            if index < 2:
+                g2x[index] = slope.astype(LOW)
             if index in (0, 2):
-                g2y[index // 2] = slope
+                g2y[index // 2] = slope.astype(LOW)
         act = gelu(pre)
         at = (x * 3 + y) * 256
         lhs3[:, at:at + 128] = act
         lhs3[:, at + 128:at + 256] = down(act, 16)
-    slopes = Halo(here, sizes, -1, halo_sems, 3, (
-        (1, 0, g2.at[pl.ds(0, 2)], g2x_in), (0, 1, g2y, g2y_in), (1, 1, g2.at[pl.ds(0, 1)], g2c_in)))
+    slopes = Halo(here, sizes, -1, halo_sems, 9, (
+        (0, 1, g2y, g2y_in), (1, 1, g2x.at[pl.ds(0, 1)], g2c_in), (1, 0, g2x, g2x_in)))
     slopes.start()
 
     others(depth, here.z, lambda q: to_cell(q, q).wait())
@@ -442,7 +445,7 @@
     pre = dot(lhs3[...].astype(LOW), third)
     delta = (gelu_slope(pre) * upstream).astype(LOW)
     d3[...] = delta
-    deltas = Halo(here, sizes, -1, halo_sems, 6, ((1, 0, d3, d3x), (0, 1, d3, d3y), (1, 1, d3, d3c)))
+    deltas = Halo(here, sizes, -1, halo_sems, 12, ((0, 1, d3, d3y), (1, 1, d3, d3c), (1, 0, d3, d3x)))
     deltas.start()
 
     for tap in range(9):
@@ -484,7 +487,7 @@
                 for from_y, dy in reads[b]:
                     at, tap = sources[from_x, from_y] * 16, (dx * 3 + dy) * 256
                     total = total + back[at:at + 16, tap:tap + 256]
-            value = slope_at[a, b][...] * (total[:, 0:128] + up(total[:, 128:256]))
+            value = slope_at[a, b][...].astype(WIDE) * (total[:, 0:128] + up(total[:, 128:256]))
             d2s[a * 3 + b, pl.ds(0, 16, stride=2), :] = value[:, 0:64]
             d2s[a * 3 + b, pl.ds(1, 16, stride=2), :] = value[:, 64:128]
 
@@ -529,27 +532,53 @@
     small.start_swap()
     large.start_depth()
     small.start_plane()
+    large.start_final()
     small.start_depth()
-    large.start_final()
     large.start_gather()
     small.start_gather()
     large.pass_on()
     small.pass_on()
-    total = large.finish()
+    sum_a[...] = large.finish()
+    sum_b[...] = small.finish()
+    volumes.sent()
+    corners.sent()
+    slopes.sent()
+    deltas.sent()
+
+
+def unpack_kernel(sum_a, sum_b, out1, out2, out3, first, second, third, sems):
     for lanes in range(2):
-        out3[:, lanes * 128:(lanes + 1) * 128] = total[lanes * 108:(lanes + 1) * 108].reshape(1728, LANES)
-    total = small.finish()
-    both = total[0:SECOND_UNITS].reshape(896, LANES)
-    out2[0:896, :] = both[:, 0:64]
-    out2[896:1728, :] = both[0:832, 64:128]
-    w1c[0:128, :] = total[SECOND_UNITS:SECOND_UNITS + FIRST_UNITS].reshape(128, LANES).astype(WIDE)
+        third[:, lanes * 128:(lanes + 1) * 128] = sum_a[lanes * 108:(lanes + 1) * 108].reshape(1728, LANES).astype(WIDE)
+    copies = [pltpu.make_async_copy(third, out3, sems.at[0])]
+    copies[0].start()
+    both = sum_b[0:SECOND_UNITS].reshape(896, LANES).astype(WIDE)
+    second[0:896, :] = both[:, 0:64]
+    second[896:1728, :] = both[0:832, 64:128]
+    copies.append(pltpu.make_async_copy(second, out2, sems.at[1]))
+    copies[1].start()
+    rows = sum_b[SECOND_UNITS:SECOND_UNITS + FIRST_UNITS].reshape(128, LANES).astype(WIDE)
     for dx in range(3):
         for dy in range(3):
             for dz in range(3):
-                out1[dx, dy, dz] = w1c[pl.ds(dz * SLOT + (dx * 3 + dy) * 4, 4), 0:64]
-    volumes.sent()
-    slopes.sent()
-    deltas.sent()
+                at = dz * SLOT + (dx * 3 + dy) * 4
+                first[dx, dy, dz] = rows[at:at + 4, 0:64]
+    copies.append(pltpu.make_async_copy(first, out1, sems.at[2]))
+    copies[2].start()
+    for move in copies:
+        move.wait()
+
+
+def unpacked(sums):
+    whole, far = pl.BlockSpec(memory_space=pltpu.VMEM), pl.BlockSpec(memory_space=pltpu.HBM)
+    shapes = ((3, 3, 3, 4, 64), (1728, 64), (1728, 256))
+    return pl.pallas_call(
+        unpack_kernel,
+        out_shape=tuple(jax.ShapeDtypeStruct(shape, WIDE) for shape in shapes),
+        in_specs=[whole] * 2,
+        out_specs=(far,) * 3,
+        scratch_shapes=[*(pltpu.VMEM(shape, WIDE) for shape in shapes), pltpu.SemaphoreType.DMA((3,))],
+        compiler_params=pltpu.CompilerParams(vmem_limit_bytes=16 * 2**20),
+    )(*sums)
 
 
 def local(sizes, volume, cotangent, first_weight, second_weight, third_weight):
@@ -564,25 +593,21 @@
     vmem, sems = pltpu.VMEM, pltpu.SemaphoreType.DMA
     mixed = CORES * min(4, size_y // CORES)
     whole, far = pl.BlockSpec(memory_space=pltpu.VMEM), pl.BlockSpec(memory_space=pltpu.HBM)
-    grads = pl.pallas_call(
+    sums = pl.pallas_call(
         functools.partial(kernel, sizes),
-        out_shape=(
-            pltpu.VMEM((3, 3, 3, 4, 64), WIDE),
-            pltpu.VMEM((1728, 64), LOW),
-            pltpu.VMEM((1728, 256), LOW),
-        ),
+        out_shape=(pltpu.VMEM((units_a, ROWS, LANES), LOW), pltpu.VMEM((units_b, ROWS, LANES), LOW)),
         in_specs=[far] * 6,
-        out_specs=(whole, whole, whole),
+        out_specs=(whole, whole),
         scratch_shapes=[
             vmem((256, 128), LOW), vmem((256, 128), LOW), vmem((256, 128), LOW), vmem((256, 128), LOW),
             vmem(cotangent.shape[1:], LOW), vmem(first_weight.shape, LOW), vmem((256, 128), WIDE), vmem((3, 3, 4, 64, 64), LOW), vmem((3, 3, 4, 64, 256), LOW), vmem((768, 896), LOW),
-            sems((8,)), sems((2, 9)),
+            sems((8,)), sems((2, 15)),
             vmem((mixed, 8, spread), WIDE), vmem((mixed, 8, spread), WIDE), sems((2, mixed)),
             vmem((depth, mixed, kept * ROWS), WIDE), vmem((depth, mixed, kept * ROWS), WIDE), sems((2, depth)),
             vmem((8, 136, 128), WIDE), vmem((5, 256, 128), LOW), vmem((7, 224, 256), LOW), vmem((4, 128, 128), WIDE),
             vmem((7, 224, 128), LOW), vmem((7, 224, 128), LOW), vmem((288, 2304), LOW), vmem((288, 64), WIDE),
-            vmem((4, 16, 128), WIDE), vmem((2, 16, 128), WIDE),
-            vmem((2, 16, 128), WIDE), vmem((2, 16, 128), WIDE), vmem((1, 16, 128), WIDE),
+            vmem((4, 16, 128), WIDE), vmem((2, 16, 128), LOW), vmem((2, 16, 128), LOW),
+            vmem((2, 16, 128), LOW), vmem((2, 16, 128), LOW), vmem((1, 16, 128), LOW),
             vmem((16, 2304), WIDE), vmem((16, 256), LOW), vmem((16, 256), LOW), vmem((16, 256), LOW), vmem((16, 256), LOW),
             vmem((2304, 128), LOW), vmem((256, 512), LOW), vmem((9, 32, 64), WIDE), vmem((512, 128), LOW),
             vmem((units_a, ROWS, LANES), WIDE), vmem((units_b, ROWS, LANES), WIDE),
@@ -591,11 +616,8 @@
         compiler_params=pltpu.CompilerParams(collective_id=1, has_side_effects=True, vmem_limit_bytes=60 * 2**20),
         cost_estimate=pl.CostEstimate(flops=1_000_000_000, bytes_accessed=8_000_000, transcendentals=1_000_000),
     )(volume.reshape(256, 128), cotangent[0], first_weight, second_weight, third_weight, jnp.asarray(selection(), LOW))
-    return (
-        grads[0],
-        grads[1].astype(WIDE).reshape(3, 3, 3, 64, 64),
-        grads[2].astype(WIDE).reshape(3, 3, 3, 64, 256),
-    )
+    first, second, third = unpacked(sums)
+    return first, second.reshape(3, 3, 3, 64, 64), third.reshape(3, 3, 3, 64, 256)
 
 
 def solution(mesh):

time: 79.5 us -> 71.7 us (0.902)
  Pallas kernels: 75.3 us -> 70.9 us
  other arithmetic: 2.42 us -> 0 us
    pallas_call x1 -> x2, Pallas kernels: 75.3 us -> 70.9 us  [the longest x1 69.2 us: local(): pl.pallas_call(functools.partial(kernel, sizes), out_shape=(pltpu.VMEM((u...]
    reshape x2 -> x0, other arithmetic: 2.42 us -> none  [the longest x1 1.41 us: local(): grads[2].astype(WIDE).reshape(3, 3, 3, 64, 256)]
where the time goes in v3:
time: 71.7 us; the launch traced here: 71.6 us
  Pallas kernels  70.9 us (99%)
    pallas_call x1, Pallas kernels, local(): pl.pallas_call(functools.partial(kernel, sizes), out_shape=(pltpu.VMEM((u...  69.2 us
    pallas_call x1, Pallas kernels, unpacked(): pl.pallas_call(unpack_kernel, out_shape=tuple((jax.ShapeDtypeStruct(shape...  1.71 us

profile of v3, /device:TPU:1, one launch (start us, length us, event | category | flops | bytes accessed | tf_op | source)
XLA Modules:
  0.0 71.6 jit_solution(15691815051783346717)
XLA Ops:
  0.6 69.2 %shard_map.85 = (bf16[224,16,128]{2,1,0:T(8,128)(2,1)S(1)}, bf16[64,16,128]{2,1,0:T(8,128)(2,1)S(1)}) custom-call(bf16[256,128]{1,0:T(8,128)(2,1)} %bitcast.6, bf16[2,8,16,16]{3,2,1,0:T(8,128)(2,1)} %bitcast.7, bf16[3,3,3,4,64]{4,3,2,1,0:T(4,128)(2,1)} %w1_hbm.1, bf16[3,3,3,64,64]{4,3,2,1,0:T(8,128)(2,1)} %w2.1, bf16[3,3,3,64,256]{4,3,2,1,0:T(8,128)(2,1)} %w3.1, ...), custom_call_target="tpu_custom_call" | custom-call | flops 1000000000 | bytes 8000000 | tf_op jit(solution)/shard_map/pallas_call | solution.py:596
  69.9 1.7 %shard_map.86 = (f32[3,3,3,4,64]{4,3,2,1,0:T(4,128)}, f32[1728,64]{1,0:T(8,128)}, f32[1728,256]{1,0:T(8,128)}) custom-call(bf16[224,16,128]{2,1,0:T(8,128)(2,1)S(1)} %get-tuple-element.8.sum_a, bf16[64,16,128]{2,1,0:T(8,128)(2,1)S(1)} %get-tuple-element.9.sum_b), custom_call_target="tpu_custom_call" | custom-call | tf_op jit(solution)/shard_map/pallas_call | solution.py:574

commit v4 on v3

--- a/solution.py
+++ b/solution.py
@@ -142,7 +142,10 @@
     def start_plane(self):
         here = self.here
         self.swap().wait()
-        mine = self.grads[pl.ds(here.core * self.half, self.half)]
+        if self.grads.shape[0] == self.half:
+            mine = self.grads[...]
+        else:
+            mine = self.grads[pl.ds(here.core * self.half, self.half)]
         self.plane_out[...] = (mine + self.half_in[...].astype(WIDE)).astype(LOW).reshape(self.plane_out.shape)
         others(here.plane, here.p, lambda q: self.to_plane(q, here.p).start())
 
@@ -342,10 +345,11 @@
             y = part * mixed + t
             s1[t, part * rows:(part + 1) * rows, :] = jnp.broadcast_to(strips[y:y + 1, :], (rows, spread))
 
+    loads[2].wait()
     pl.semaphore_wait(barrier, expected)
     pieces = [pl.ds(64 * channel, 64) for channel in range(4)]
     volumes = Halo(here, sizes, 1, halo_sems, 0, (
-        *((0, 1, volume_hbm.at[piece], vy.at[piece]) for piece in pieces), (1, 0, volume_hbm, vx)))
+        *((0, 1, volume.at[piece], vy.at[piece]) for piece in pieces), (1, 0, volume, vx)))
     corners = Halo(here, sizes, 1, halo_sems, 5, [(1, 0, vy.at[piece], vc.at[piece]) for piece in pieces], here.sy > 0)
     volumes.start()
 
@@ -368,8 +372,7 @@
     for part in range(4):
         volumes.wait(part, part + 1)
         corners.start(part, part + 1)
-    for load in loads[2:4]:
-        load.wait()
+    loads[3].wait()
     volumes.wait(4)
     corners.wait()
 
@@ -448,20 +451,26 @@
     deltas = Halo(here, sizes, -1, halo_sems, 12, ((0, 1, d3, d3y), (1, 1, d3, d3c), (1, 0, d3, d3x)))
     deltas.start()
 
-    for tap in range(9):
-        turned = lhs3[:, tap * 256:(tap + 1) * 256].T.astype(LOW)
-        grad = dot(turned, delta)
-        for dz, rows in enumerate((192, 0, 64)):
-            for lanes in range(2):
-                at = lanes * 108 + (tap * 3 + dz) * 4
-                grads_a[at:at + 4] = grad[rows:rows + 64, lanes * 128:(lanes + 1) * 128].reshape(4, ROWS, LANES)
-    spare = grads_a.shape[0] - THIRD_UNITS
-    if spare:
-        grads_a[THIRD_UNITS:] = jnp.zeros((spare, ROWS, LANES), WIDE)
     many = len(reductions) // 2
     large = Reduction(here, grads_a, reductions[:many], False)
     small = Reduction(here, grads_b, reductions[many:], True)
-    large.start_swap()
+    turned = [lhs3[:, tap * 256:(tap + 1) * 256].T.astype(LOW) for tap in range(9)]
+    halves = [delta[:, lanes * 128:(lanes + 1) * 128].astype(WIDE) for lanes in range(2)]
+    even = here.core == 0
+
+    def third_grad(right, target):
+        for tap in range(9):
+            grad = dot(turned[tap], right.astype(LOW))
+            for dz, rows in enumerate((192, 0, 64)):
+                at = (tap * 3 + dz) * 4
+                target[at:at + 4] = grad[rows:rows + 64].astype(target.dtype).reshape(4, ROWS, LANES)
+        spare = target.shape[0] - THIRD_UNITS // 2
+        if spare:
+            target[THIRD_UNITS // 2:] = jnp.zeros((spare, ROWS, LANES), target.dtype)
+
+    third_grad(jnp.where(even, halves[1], halves[0]), large.half_out)
+    large.swap().start()
+    third_grad(jnp.where(even, halves[0], halves[1]), grads_a)
 
     for block in range(18):
         lhs2t[block * 128:(block + 1) * 128, :] = lhs2[0:128, block * 128:(block + 1) * 128].astype(WIDE).T.astype(LOW)
@@ -547,23 +556,29 @@
 
 
 def unpack_kernel(sum_a, sum_b, out1, out2, out3, first, second, third, sems):
-    for lanes in range(2):
-        third[:, lanes * 128:(lanes + 1) * 128] = sum_a[lanes * 108:(lanes + 1) * 108].reshape(1728, LANES).astype(WIDE)
-    copies = [pltpu.make_async_copy(third, out3, sems.at[0])]
-    copies[0].start()
+    half = sum_a.shape[0] // 2
+    copies = []
+    for part in range(3):
+        for lanes in range(2):
+            at = lanes * half + part * 36
+            block = sum_a[at:at + 36].reshape(576, LANES)
+            third[part * 576:(part + 1) * 576, lanes * 128:(lanes + 1) * 128] = block.astype(WIDE)
+        rows = pl.ds(part * 576, 576)
+        copies.append(pltpu.make_async_copy(third.at[rows], out3.at[rows], sems.at[part]))
+        copies[part].start()
     both = sum_b[0:SECOND_UNITS].reshape(896, LANES).astype(WIDE)
     second[0:896, :] = both[:, 0:64]
     second[896:1728, :] = both[0:832, 64:128]
-    copies.append(pltpu.make_async_copy(second, out2, sems.at[1]))
-    copies[1].start()
+    copies.append(pltpu.make_async_copy(second, out2, sems.at[3]))
+    copies[3].start()
     rows = sum_b[SECOND_UNITS:SECOND_UNITS + FIRST_UNITS].reshape(128, LANES).astype(WIDE)
     for dx in range(3):
         for dy in range(3):
             for dz in range(3):
                 at = dz * SLOT + (dx * 3 + dy) * 4
                 first[dx, dy, dz] = rows[at:at + 4, 0:64]
-    copies.append(pltpu.make_async_copy(first, out1, sems.at[2]))
-    copies[2].start()
+    copies.append(pltpu.make_async_copy(first, out1, sems.at[4]))
+    copies[4].start()
     for move in copies:
         move.wait()
 
@@ -576,7 +591,7 @@
         out_shape=tuple(jax.ShapeDtypeStruct(shape, WIDE) for shape in shapes),
         in_specs=[whole] * 2,
         out_specs=(far,) * 3,
-        scratch_shapes=[*(pltpu.VMEM(shape, WIDE) for shape in shapes), pltpu.SemaphoreType.DMA((3,))],
+        scratch_shapes=[*(pltpu.VMEM(shape, WIDE) for shape in shapes), pltpu.SemaphoreType.DMA((5,))],
         compiler_params=pltpu.CompilerParams(vmem_limit_bytes=16 * 2**20),
     )(*sums)
 
@@ -610,7 +625,7 @@
             vmem((2, 16, 128), LOW), vmem((2, 16, 128), LOW), vmem((1, 16, 128), LOW),
             vmem((16, 2304), WIDE), vmem((16, 256), LOW), vmem((16, 256), LOW), vmem((16, 256), LOW), vmem((16, 256), LOW),
             vmem((2304, 128), LOW), vmem((256, 512), LOW), vmem((9, 32, 64), WIDE), vmem((512, 128), LOW),
-            vmem((units_a, ROWS, LANES), WIDE), vmem((units_b, ROWS, LANES), WIDE),
+            vmem((units_a // 2, ROWS, LANES), WIDE), vmem((units_b, ROWS, LANES), WIDE),
             *Reduction.scratch(units_a, plane, depth, False), *Reduction.scratch(units_b, plane, depth, True),
         ],
         compiler_params=pltpu.CompilerParams(collective_id=1, has_side_effects=True, vmem_limit_bytes=60 * 2**20),

time: 71.7 us -> 71.2 us (level)
  no operation moved by 1% of the time
where the time goes in v4:
time: 71.2 us; the launch traced here: 71.1 us
  Pallas kernels  70.5 us (99%)
    pallas_call x1, Pallas kernels, local(): pl.pallas_call(functools.partial(kernel, sizes), out_shape=(pltpu.VMEM((u...  68.9 us
    pallas_call x1, Pallas kernels, unpacked(): pl.pallas_call(unpack_kernel, out_shape=tuple((jax.ShapeDtypeStruct(shape...  1.62 us

profile of v4, /device:TPU:1, one launch (start us, length us, event | category | flops | bytes accessed | tf_op | source)
XLA Modules:
  0.0 71.1 jit_solution(15977398402258860328)
XLA Ops:
  0.6 68.9 %shard_map.85 = (bf16[224,16,128]{2,1,0:T(8,128)(2,1)S(1)}, bf16[64,16,128]{2,1,0:T(8,128)(2,1)S(1)}) custom-call(bf16[256,128]{1,0:T(8,128)(2,1)} %bitcast.6, bf16[2,8,16,16]{3,2,1,0:T(8,128)(2,1)} %bitcast.7, bf16[3,3,3,4,64]{4,3,2,1,0:T(4,128)(2,1)} %w1_hbm.1, bf16[3,3,3,64,64]{4,3,2,1,0:T(8,128)(2,1)} %w2.1, bf16[3,3,3,64,256]{4,3,2,1,0:T(8,128)(2,1)} %w3.1, ...), custom_call_target="tpu_custom_call" | custom-call | flops 1000000000 | bytes 8000000 | tf_op jit(solution)/shard_map/pallas_call | solution.py:611
  69.5 1.6 %shard_map.86 = (f32[3,3,3,4,64]{4,3,2,1,0:T(4,128)}, f32[1728,64]{1,0:T(8,128)}, f32[1728,256]{1,0:T(8,128)}) custom-call(bf16[224,16,128]{2,1,0:T(8,128)(2,1)S(1)} %get-tuple-element.8.sum_a, bf16[64,16,128]{2,1,0:T(8,128)(2,1)S(1)} %get-tuple-element.9.sum_b), custom_call_target="tpu_custom_call" | custom-call | tf_op jit(solution)/shard_map/pallas_call | solution.py:589

commit v5 on v4

--- a/solution.py
+++ b/solution.py
@@ -303,7 +303,7 @@
     others(mixed, here.t, lambda q: greet(at_mixed(q)))
     others(here.plane, here.p, lambda q: greet(here.device(p=q)))
     loads = [
-        pltpu.make_async_copy(w1_hbm, w1, local_sems.at[0]),
+        pltpu.make_async_copy(w1_hbm, w1.at[pl.ds(0, 3)], local_sems.at[0]),
         pltpu.make_async_copy(cotangent_hbm, cotangent, local_sems.at[1]),
         pltpu.make_async_copy(volume_hbm, volume, local_sems.at[2]),
         pltpu.make_async_copy(select, sel, local_sems.at[3]),
@@ -577,7 +577,7 @@
             for dz in range(3):
                 at = dz * SLOT + (dx * 3 + dy) * 4
                 first[dx, dy, dz] = rows[at:at + 4, 0:64]
-    copies.append(pltpu.make_async_copy(first, out1, sems.at[4]))
+    copies.append(pltpu.make_async_copy(first.at[pl.ds(0, 3)], out1, sems.at[4]))
     copies[4].start()
     for move in copies:
         move.wait()
@@ -591,7 +591,7 @@
         out_shape=tuple(jax.ShapeDtypeStruct(shape, WIDE) for shape in shapes),
         in_specs=[whole] * 2,
         out_specs=(far,) * 3,
-        scratch_shapes=[*(pltpu.VMEM(shape, WIDE) for shape in shapes), pltpu.SemaphoreType.DMA((5,))],
+        scratch_shapes=[*(pltpu.VMEM(shape, WIDE) for shape in ((4, *shapes[0][1:]), *shapes[1:])), pltpu.SemaphoreType.DMA((5,))],
         compiler_params=pltpu.CompilerParams(vmem_limit_bytes=16 * 2**20),
     )(*sums)
 
@@ -615,7 +615,7 @@
         out_specs=(whole, whole),
         scratch_shapes=[
             vmem((256, 128), LOW), vmem((256, 128), LOW), vmem((256, 128), LOW), vmem((256, 128), LOW),
-            vmem(cotangent.shape[1:], LOW), vmem(first_weight.shape, LOW), vmem((256, 128), WIDE), vmem((3, 3, 4, 64, 64), LOW), vmem((3, 3, 4, 64, 256), LOW), vmem((768, 896), LOW),
+            vmem(cotangent.shape[1:], LOW), vmem((4, *first_weight.shape[1:]), LOW), vmem((256, 128), WIDE), vmem((3, 3, 4, 64, 64), LOW), vmem((3, 3, 4, 64, 256), LOW), vmem((768, 896), LOW),
             sems((8,)), sems((2, 15)),
             vmem((mixed, 8, spread), WIDE), vmem((mixed, 8, spread), WIDE), sems((2, mixed)),
             vmem((depth, mixed, kept * ROWS), WIDE), vmem((depth, mixed, kept * ROWS), WIDE), sems((2, depth)),

time: 71.2 us -> 71.3 us (level)
  no operation moved by 1% of the time
where the time goes in v5:
time: 71.3 us; the launch traced here: 71.1 us
  Pallas kernels  70.5 us (99%)
    pallas_call x1, Pallas kernels, local(): pl.pallas_call(functools.partial(kernel, sizes), out_shape=(pltpu.VMEM((u...  68.9 us
    pallas_call x1, Pallas kernels, unpacked(): pl.pallas_call(unpack_kernel, out_shape=tuple((jax.ShapeDtypeStruct(shape...  1.62 us

profile of v5, /device:TPU:1, one launch (start us, length us, event | category | flops | bytes accessed | tf_op | source)
XLA Modules:
  0.0 71.1 jit_solution(13265968047859384892)
XLA Ops:
  0.6 68.9 %shard_map.85 = (bf16[224,16,128]{2,1,0:T(8,128)(2,1)S(1)}, bf16[64,16,128]{2,1,0:T(8,128)(2,1)S(1)}) custom-call(bf16[256,128]{1,0:T(8,128)(2,1)} %bitcast.6, bf16[2,8,16,16]{3,2,1,0:T(8,128)(2,1)} %bitcast.7, bf16[3,3,3,4,64]{4,3,2,1,0:T(4,128)(2,1)} %w1_hbm.1, bf16[3,3,3,64,64]{4,3,2,1,0:T(8,128)(2,1)} %w2.1, bf16[3,3,3,64,256]{4,3,2,1,0:T(8,128)(2,1)} %w3.1, ...), custom_call_target="tpu_custom_call" | custom-call | flops 1000000000 | bytes 8000000 | tf_op jit(solution)/shard_map/pallas_call | solution.py:611
  69.5 1.6 %shard_map.86 = (f32[3,3,3,4,64]{4,3,2,1,0:T(4,128)}, f32[1728,64]{1,0:T(8,128)}, f32[1728,256]{1,0:T(8,128)}) custom-call(bf16[224,16,128]{2,1,0:T(8,128)(2,1)S(1)} %get-tuple-element.8.sum_a, bf16[64,16,128]{2,1,0:T(8,128)(2,1)S(1)} %get-tuple-element.9.sum_b), custom_call_target="tpu_custom_call" | custom-call | tf_op jit(solution)/shard_map/pallas_call | solution.py:589
